TPU v7x, 128 devices: a whole 4x4x4 slice. The times are simulated.
128 devices in a mesh: gx: 8 (over y_lo, z), gy: 16 (over x, y_hi, core).
Axes of the slice: x: 4, y: 4 (y_hi: 2, y_lo: 2; y = y_hi * 2 + y_lo), z: 4, core: 2. Of those that a mesh axis runs over, the one named last changes fastest.
Arguments:
- matrix: float32 [262144, 512], P(('gx', 'gy'))
- sign_flips: int32 [262144], P(('gx', 'gy')), may hold values from -1 to 1, as said below
- sampled_rows: int32 [32768], P(('gx', 'gy')), may hold values from 0 to 2047, as said below
Outputs:
- gram: float32 [512, 512], P(('gx', 'gy'))
Inputs may be any that keep to these rules, and one draw needn't show every extreme that they name: `sign_flips`: each entry is -1 or +1. `sampled_rows`: within each aligned block of 256 entries the offsets are distinct and ascending; block b refers to rows b * 2048 onward.
All inputs are finite; a program needn't handle non-finite values.
Results may differ from a plain program's by a relative error of at most 0.00005.
Values sent between devices are 32-bit elements; how exact they have to be, the bound alone decides.
No kernel may reach another device: no remote copies, remote signals or barrier semaphores. Data moves between devices by JAX's collectives and lax.ppermute only.
A program may use at most 64 MiB of HBM per device.

v0:
```python
import math

import jax
import jax.numpy as jnp
from jax import lax
from jax.sharding import PartitionSpec as P


def partner_2(value, axis, bit):
    mask = 2**bit
    pairs = [(source, source ^ mask) for source in range(lax.axis_size(axis))]
    return lax.ppermute(value, axis, pairs)


def sign_table(order):
    counter = lax.iota(jnp.int32, order)
    shared = jnp.bitwise_and(counter[:, None], counter[None, :])
    parity = jnp.zeros((order, order), jnp.int32)
    for level in range(order.bit_length() - 1):
        parity = parity + jnp.bitwise_and(jnp.right_shift(shared, level), 1)
    return jnp.where(parity % 2 == 0, 1.0, -1.0).astype(jnp.float32)


def outer_sum(left, right):
    return lax.dot_general(
        left,
        right,
        (((0,), (0,)), ((), ())),
        precision=lax.Precision.HIGHEST,
        preferred_element_type=jnp.float32,
    )


def butterfly(current, axis_name, position, partner):
    upper = position // (1 << axis_name) % 2
    return jnp.where(upper == 1, partner - current, current + partner)


def local(matrix, sign_flips, sampled_rows):
    row_count = matrix.shape[0]
    across_x = lax.axis_size("gx")
    across_y = lax.axis_size("gy")
    device_count = across_x * across_y
    factor = 1.0 / math.sqrt(row_count * device_count)
    sample_total = sampled_rows.shape[0] * device_count
    signed = matrix * sign_flips.astype(jnp.float32)[:, None]
    mixed = jnp.dot(
        sign_table(row_count),
        signed,
        precision=lax.Precision.HIGHEST,
        preferred_element_type=jnp.float32,
    )
    current = mixed
    index_y = lax.axis_index("gy")
    for level in range(across_y.bit_length() - 1):
        partner = partner_2(current, "gy", level)
        current = butterfly(current, level, index_y, partner)
    index_x = lax.axis_index("gx")
    for level in range(across_x.bit_length() - 1):
        partner = partner_2(current, "gx", level)
        current = butterfly(current, level, index_x, partner)
    transformed = current * factor
    picked = jnp.take(transformed, sampled_rows, axis=0)
    term = outer_sum(picked, picked) * (1.0 / sample_total)
    return lax.psum_scatter(term, ("gx", "gy"), scatter_dimension=0, tiled=True)


def solution(mesh):
    placed = (P(("gx", "gy"), None), P(("gx", "gy")), P(("gx", "gy")))
    return jax.shard_map(
        local, mesh=mesh, in_specs=placed, out_specs=P(("gx", "gy"), None), check_vma=False
    )
```

profile of v0, /device:TPU:0, one launch (start us, length us, event | category | flops | bytes accessed | tf_op | source)
XLA Modules:
  0.0 1041.4 jit_solution(7143319393896289813)
XLA Ops:
  6.5 0.0 all-reduce.3.cloned.1.call-start
  6.5 0.7 convert_element_type.3
  7.2 2.5 fusion.46
  9.8 266.9 %fusion.2 = f32[2048,512]{1,0:T(8,128)} fusion(f32[2048,512]{1,0:T(8,128)S(1)} %fusion.46), kind=kOutput, calls=%fused_computation.6 | convolution fusion | flops 25962741760 | bytes 8388608 | tf_op jit(solution)/shard_map/dot_general | solution.py:47
  276.7 0.0 collective-permute-start
  276.7 7.5 collective-permute-done
  284.2 6.5 add_select_fusion.6
  290.7 3.3 collective-permute-start.1
  293.9 91.2 %collective-permute-done.1 = f32[2048,512]{1,0:T(8,128)} collective-permute-done((f32[2048,512]{1,0:T(8,128)}, f32[2048,512]{1,0:T(8,128)}, u32[]{:S(2)}, u32[]{:S(2)}) %collective-permute-start.1) | collective-permute-done | bytes 4194336 | tf_op jit(solution)/shard_map/ppermute | solution.py:12
  385.1 6.5 add_select_fusion.5
  391.6 1.5 collective-permute-start.2
  393.1 90.6 %collective-permute-done.2 = f32[2048,512]{1,0:T(8,128)} collective-permute-done((f32[2048,512]{1,0:T(8,128)}, f32[2048,512]{1,0:T(8,128)}, u32[]{:S(2)}, u32[]{:S(2)}) %collective-permute-start.2) | collective-permute-done | bytes 4194336 | tf_op jit(solution)/shard_map/ppermute | solution.py:12
  483.7 6.5 add_select_fusion.4
  490.2 3.0 collective-permute-start.3
  493.3 89.7 %collective-permute-done.3 = f32[2048,512]{1,0:T(8,128)} collective-permute-done((f32[2048,512]{1,0:T(8,128)}, f32[2048,512]{1,0:T(8,128)}, u32[]{:S(2)}, u32[]{:S(2)}) %collective-permute-start.3) | collective-permute-done | bytes 4194336 | tf_op jit(solution)/shard_map/ppermute | solution.py:12
  583.0 6.5 add_select_fusion.3
  589.4 1.9 collective-permute-start.4
  591.3 88.5 %collective-permute-done.4 = f32[2048,512]{1,0:T(8,128)} collective-permute-done((f32[2048,512]{1,0:T(8,128)}, f32[2048,512]{1,0:T(8,128)}, u32[]{:S(2)}, u32[]{:S(2)}) %collective-permute-start.4) | collective-permute-done | bytes 4194336 | tf_op jit(solution)/shard_map/ppermute | solution.py:12
  679.9 6.5 add_select_fusion.2
  686.4 3.7 collective-permute-start.5
  690.0 0.0 copy-start
  690.1 87.6 %collective-permute-done.5 = f32[2048,512]{1,0:T(8,128)} collective-permute-done((f32[2048,512]{1,0:T(8,128)}, f32[2048,512]{1,0:T(8,128)}, u32[]{:S(2)}, u32[]{:S(2)}) %collective-permute-start.5) | collective-permute-done | bytes 4194336 | tf_op jit(solution)/shard_map/ppermute | solution.py:12
  777.6 6.5 add_select_fusion.1
  784.1 1.6 collective-permute-start.6
  785.7 0.0 copy-done
  785.7 87.1 %collective-permute-done.6 = f32[2048,512]{1,0:T(8,128)} collective-permute-done((f32[2048,512]{1,0:T(8,128)}, f32[2048,512]{1,0:T(8,128)}, u32[]{:S(2)}, u32[]{:S(2)}) %collective-permute-start.6) | collective-permute-done | bytes 4194336 | tf_op jit(solution)/shard_map/ppermute | solution.py:12
  872.8 6.5 select_multiply_fusion
  879.3 3.4 gather_fusion
  882.7 2.2 convolution_multiply_fusion
  884.9 0.0 all-reduce.3.cloned.1.call-update
  885.0 148.3 %all-reduce.3.cloned.1.call-done = f32[512,512]{1,0:T(8,128)} async-done(((f32[512,512]{1,0:T(8,128)}), f32[512,512]{1,0:T(8,128)}) %all-reduce.3.cloned.1.call-update) | async-done | bytes 1048592
  1033.3 1.3 constant_dynamic-slice_fusion
  (3 shorter events, 0.0 us)
Async XLA Ops:
  6.5 1026.7 %all-reduce.3.cloned.1.call-start = ((), (), s32[]{:S(2)}) async-start(), calls=%async_computation | async-start | bytes 2097152
  276.7 7.5 collective-permute-start
  290.7 94.5 %collective-permute-start.1 = (f32[2048,512]{1,0:T(8,128)}, f32[2048,512]{1,0:T(8,128)}, u32[]{:S(2)}, u32[]{:S(2)}) collective-permute-start(f32[2048,512]{1,0:T(8,128)} %add_select_fusion.6), channel_id=1, source_target_pairs={{0,2},{1,3},{2,0},{3,1},{4,6},{5,7},{6,4},{7,5},{8,10},{9,11},{10,... | collective-permute-start | bytes 12582920 | tf_op jit(solution)/shard_map/ppermute | solution.py:12
  391.6 92.1 %collective-permute-start.2 = (f32[2048,512]{1,0:T(8,128)}, f32[2048,512]{1,0:T(8,128)}, u32[]{:S(2)}, u32[]{:S(2)}) collective-permute-start(f32[2048,512]{1,0:T(8,128)} %add_select_fusion.5), channel_id=1, source_target_pairs={{0,4},{1,5},{2,6},{3,7},{4,0},{5,1},{6,2},{7,3},{8,12},{9,13},{10,... | collective-permute-start | bytes 12582920 | tf_op jit(solution)/shard_map/ppermute | solution.py:12
  490.2 92.7 %collective-permute-start.3 = (f32[2048,512]{1,0:T(8,128)}, f32[2048,512]{1,0:T(8,128)}, u32[]{:S(2)}, u32[]{:S(2)}) collective-permute-start(f32[2048,512]{1,0:T(8,128)} %add_select_fusion.4), channel_id=1, source_target_pairs={{0,8},{1,9},{2,10},{3,11},{4,12},{5,13},{6,14},{7,15},{8,0},{9,1},... | collective-permute-start | bytes 12582920 | tf_op jit(solution)/shard_map/ppermute | solution.py:12
  589.4 90.4 %collective-permute-start.4 = (f32[2048,512]{1,0:T(8,128)}, f32[2048,512]{1,0:T(8,128)}, u32[]{:S(2)}, u32[]{:S(2)}) collective-permute-start(f32[2048,512]{1,0:T(8,128)} %add_select_fusion.3), channel_id=1, source_target_pairs={{0,16},{16,0},{32,48},{48,32},{64,80},{80,64},{96,112},{112,96},{1... | collective-permute-start | bytes 12582920 | tf_op jit(solution)/shard_map/ppermute | solution.py:12
  686.4 91.3 %collective-permute-start.5 = (f32[2048,512]{1,0:T(8,128)}, f32[2048,512]{1,0:T(8,128)}, u32[]{:S(2)}, u32[]{:S(2)}) collective-permute-start(f32[2048,512]{1,0:T(8,128)} %add_select_fusion.2), channel_id=1, source_target_pairs={{0,32},{16,48},{32,0},{48,16},{64,96},{80,112},{96,64},{112,80},{1... | collective-permute-start | bytes 12582920 | tf_op jit(solution)/shard_map/ppermute | solution.py:12
  690.0 95.7 %copy-start = (s32[256]{0:T(256)S(1)}, s32[256]{0:T(256)}, u32[]{:S(2)}) copy-start(s32[256]{0:T(256)} %param.5) | copy-start | bytes 3076
  784.1 88.7 %collective-permute-start.6 = (f32[2048,512]{1,0:T(8,128)}, f32[2048,512]{1,0:T(8,128)}, u32[]{:S(2)}, u32[]{:S(2)}) collective-permute-start(f32[2048,512]{1,0:T(8,128)} %add_select_fusion.1), channel_id=1, source_target_pairs={{0,64},{16,80},{32,96},{48,112},{64,0},{80,16},{96,32},{112,48},{1... | collective-permute-start | bytes 12582920 | tf_op jit(solution)/shard_map/ppermute | solution.py:12
Sparse Core Ops, SparseCore 0:
  885.1 148.1 all-reduce.2
where the time goes:
time: 1040 us
  waiting for transfers between devices  690 us (66%)
  matrix products  269 us (26%)
  other arithmetic  48.7 us (5%)
  starting transfers between devices  15 us (1%)
  between operations  13.4 us (1%)
    ppermute x7, waiting for transfers between devices, partner_2(): return lax.ppermute(value, axis, pairs)  542 us
    dot_general x1, matrix products, local(): jnp.dot(sign_table(row_count), signed, precision=lax.Precision.HIGHEST, p...  267 us
    unnamed x2, waiting for transfers between devices  148 us
    select_n x6, other arithmetic, butterfly(): return jnp.where(upper == 1, partner - current, current + partner)  38.9 us
  transfers between devices with their start and end apart: 8, of which 8 were waited for; matrix products, arithmetic and copies ran while one was open for 0% of the time, Pallas kernels for 0%

commit v1 on v0

v1 whole, which is shorter than its diff:
```python
import jax
import jax.numpy as jnp
import numpy as np
from jax import lax
from jax.experimental import pallas as pl
from jax.experimental.pallas import tpu as pltpu
from jax.sharding import Mesh, PartitionSpec as P

AXES = ("yl", "z", "x", "yh", "c")
CHIPS = ("yl", "z", "x", "yh")
TILE = 256
LANES = 128


def hadamard(order):
    grid = np.arange(order)[:, None] & np.arange(order)[None, :]
    parity = np.zeros((order, order), np.int32)
    for bit in range(order.bit_length() - 1):
        parity ^= (grid >> bit) & 1
    return 1.0 - 2.0 * parity


def butterfly(value):
    count = value.shape[0]
    if count == 1:
        return value
    half = count // 2
    first, second = value[:half], value[half:]
    return jnp.concatenate([butterfly(first + second), butterfly(first - second)])


def split2(value):
    high = value.astype(jnp.bfloat16)
    low = (value - high.astype(jnp.float32)).astype(jnp.bfloat16)
    return high, low


def split3(value):
    high = value.astype(jnp.bfloat16)
    rest = value - high.astype(jnp.float32)
    middle = rest.astype(jnp.bfloat16)
    low = (rest - middle.astype(jnp.float32)).astype(jnp.bfloat16)
    return high, middle, low


def mix_kernel(signs, table, block, mixed):
    groups = signs.shape[0]
    width = block.shape[1]
    for group in range(groups):
        rows = pl.ds(group * TILE, TILE)
        left = (table[...] * signs[group : group + 1, :]).astype(jnp.bfloat16)
        high, middle, low = split3(block[rows, :])
        mixed[rows, :] = (
            jnp.dot(left, low, preferred_element_type=jnp.float32)
            + jnp.dot(left, middle, preferred_element_type=jnp.float32)
            + jnp.dot(left, high, preferred_element_type=jnp.float32)
        )
    for start in range(0, TILE, 8):
        for lane in range(0, width, LANES):
            value = jnp.stack(
                [mixed[group * TILE + start : group * TILE + start + 8, lane : lane + LANES] for group in range(groups)]
            )
            value = butterfly(value)
            for group in range(groups):
                mixed[group * TILE + start : group * TILE + start + 8, lane : lane + LANES] = value[group]


def local_mix(matrix, signs):
    rows, columns = matrix.shape
    groups = rows // TILE
    width = 256
    return pl.pallas_call(
        mix_kernel,
        grid=(columns // width,),
        out_shape=jax.ShapeDtypeStruct((rows, columns), jnp.float32),
        in_specs=[
            pl.BlockSpec((groups, TILE), lambda i: (0, 0)),
            pl.BlockSpec((TILE, TILE), lambda i: (0, 0)),
            pl.BlockSpec((rows, width), lambda i: (0, i)),
        ],
        out_specs=pl.BlockSpec((rows, width), lambda i: (0, i)),
        compiler_params=pltpu.CompilerParams(vmem_limit_bytes=48 << 20),
        cost_estimate=pl.CostEstimate(flops=2 * rows * TILE * columns * 3, bytes_accessed=8 * rows * columns, transcendentals=0),
        name="local_mix",
    )(signs.reshape(groups, TILE).astype(jnp.float32), jnp.asarray(hadamard(TILE), jnp.float32), matrix)


def gram_kernel(scale, block, chosen, gram, work, parts):
    devices, inner, columns = block.shape
    near = 8
    far = devices // near
    for lane in range(0, columns, LANES):
        lanes = pl.ds(lane, LANES)
        for tile in range(0, inner, 8):
            sub = pl.ds(tile, 8)
            for start in range(near):
                value = jnp.stack([block[start + near * step, sub, lanes] for step in range(far)])
                value = butterfly(value)
                for step in range(far):
                    work[start + near * step] = value[step]
            for step in range(far):
                value = butterfly(work[near * step : near * (step + 1)])
                value = value * chosen[near * step : near * (step + 1), sub, :]
                value = value.reshape(near * 8, LANES)
                high, low = split2(value)
                base = (tile // 8 * devices + near * step) * 8
                parts[pl.ds(base, near * 8), lanes] = high
                parts[pl.ds(base, near * 8), pl.ds(columns + lane, LANES)] = low
    product = lax.dot_general(
        parts[:, :columns], parts[...], (((0,), (0,)), ((), ())), preferred_element_type=jnp.float32
    )
    cross = product[:, columns:]
    gram[...] = (product[:, :columns] + (cross + cross.T)) * scale


def local_gram(block, chosen, scale):
    devices, inner, columns = block.shape
    whole = lambda *shape: pl.BlockSpec(shape, lambda: (0,) * len(shape))
    rows = devices * inner
    return pl.pallas_call(
        lambda *refs: gram_kernel(scale, *refs),
        out_shape=jax.ShapeDtypeStruct((columns, columns), jnp.float32),
        in_specs=[whole(devices, inner, columns), whole(devices, inner, LANES)],
        out_specs=whole(columns, columns),
        scratch_shapes=[
            pltpu.VMEM((devices, 8, LANES), jnp.float32),
            pltpu.VMEM((rows, 2 * columns), jnp.bfloat16),
        ],
        compiler_params=pltpu.CompilerParams(vmem_limit_bytes=48 << 20),
        cost_estimate=pl.CostEstimate(flops=4 * rows * columns * columns, bytes_accessed=4 * rows * columns, transcendentals=0),
        name="local_gram",
    )(block, chosen)


def swap_core(value):
    return lax.ppermute(value, "c", [(0, 1), (1, 0)])


def local(matrix, sign_flips, sampled_rows):
    rows, columns = matrix.shape
    devices = lax.axis_size(AXES)
    chips = devices // 2
    inner = rows // devices
    samples = sampled_rows.shape[0] * devices
    scale = 1.0 / (rows * devices) / samples

    mixed = local_mix(matrix, sign_flips)
    hits = sampled_rows[None, :] == lax.iota(jnp.int32, rows)[:, None]
    flags = jnp.max(hits.astype(jnp.float32), axis=1).reshape(devices, inner)
    blocks = lax.all_to_all(mixed, AXES, 0, 0, tiled=True)
    flags = lax.all_to_all(flags, AXES, 0, 0, tiled=True)
    chosen = jnp.broadcast_to(flags[:, :, None], (devices, inner, LANES))
    partial = local_gram(blocks.reshape(devices, inner, columns), chosen, scale)

    core = lax.axis_index("c")
    out_rows = columns // devices
    halves = partial.reshape(chips, 2, out_rows, columns)
    mine = lax.dynamic_index_in_dim(halves, core, 1, keepdims=False)
    other = lax.dynamic_index_in_dim(halves, 1 - core, 1, keepdims=False)
    summed = mine + swap_core(other)
    pieces = lax.all_to_all(summed, CHIPS, 0, 0, tiled=True)
    return jnp.sum(pieces, axis=0)


def solution(mesh):
    fine = Mesh(mesh.devices.reshape(2, 4, 4, 2, 2), AXES)
    return jax.shard_map(
        local, mesh=fine, in_specs=(P(AXES, None), P(AXES), P(AXES)), out_specs=P(AXES, None), check_vma=False
    )
```

time: 1040 us -> 114 us (0.11)
  waiting for transfers between devices: 690 us -> 53.5 us
  matrix products: 269 us -> 0 us
  other arithmetic: 48.7 us -> 2.6 us
  blocking collectives: 0 us -> 21.7 us
  between operations: 13.4 us -> 0.07 us
  Pallas kernels: 0 us -> 10.9 us
    ppermute x7 -> x1, waiting for transfers between devices: 542 us -> 1.54 us  [swap_core(): return lax.ppermute(value, 'c', [(0, 1), (1, 0)])]
    dot_general x2 -> x0, matrix products: 269 us -> none  [the longest x1 267 us: local(): jnp.dot(sign_table(row_count), signed, precision=lax.Precision.HIGHEST, p...]
    unnamed x2 -> x0, waiting for transfers between devices: 148 us -> none
    all_to_all x0 -> x2, waiting for transfers between devices: none -> 52 us  [the longest x1 50.8 us: local(): blocks = lax.all_to_all(mixed, AXES, 0, 0, tiled=True)]
    select_n x7 -> x0, other arithmetic: 38.9 us -> none  [the longest x6 38.9 us: butterfly(): return jnp.where(upper == 1, partner - current, current + partner)]
    all_to_all x0 -> x1, blocking collectives: none -> 21.7 us  [local(): pieces = lax.all_to_all(summed, CHIPS, 0, 0, tiled=True)]
    all_to_all x0 -> x2, starting transfers between devices: none -> 20.3 us  [the longest x1 11.1 us: local(): flags = lax.all_to_all(flags, AXES, 0, 0, tiled=True)]
    ppermute x7 -> x1, starting transfers between devices: 15 us -> 0.72 us  [swap_core(): return lax.ppermute(value, 'c', [(0, 1), (1, 0)])]
  transfers between devices with their start and end apart: 8 -> 3, of which waited for: 8 -> 3; matrix products, arithmetic and copies ran while one was open for 0% -> 1% of each run, Pallas kernels for 0% -> 4%
where the time goes in v1:
time: 114 us
  waiting for transfers between devices  53.5 us (47%)
  blocking collectives  21.7 us (19%)
  starting transfers between devices  21 us (18%)
  Pallas kernels  10.9 us (10%)
  local copies, waits for them, and re-layouts  4.28 us (4%)
  other arithmetic  2.6 us (2%)
    all_to_all x1, waiting for transfers between devices, local(): blocks = lax.all_to_all(mixed, AXES, 0, 0, tiled=True)  50.8 us
    all_to_all x1, blocking collectives, local(): pieces = lax.all_to_all(summed, CHIPS, 0, 0, tiled=True)  21.7 us
    all_to_all x1, starting transfers between devices, local(): flags = lax.all_to_all(flags, AXES, 0, 0, tiled=True)  11.1 us
    all_to_all x1, starting transfers between devices, local(): blocks = lax.all_to_all(mixed, AXES, 0, 0, tiled=True)  9.13 us
    pallas_call x1, Pallas kernels, local_gram(): pl.pallas_call(lambda *refs: gram_kernel(scale, *refs), out_shape=jax.Sha...  6.58 us
    pallas_call x1, Pallas kernels, local_mix(): pl.pallas_call(mix_kernel, grid=(columns // width,), out_shape=jax.ShapeD...  4.34 us
    unnamed x4, local copies, waits for them, and re-layouts  2.88 us
  transfers between devices with their start and end apart: 3, of which 3 were waited for; matrix products, arithmetic and copies ran while one was open for 1% of the time, Pallas kernels for 4%

profile of v1, /device:TPU:0, one launch (start us, length us, event | category | flops | bytes accessed | tf_op | source)
XLA Modules:
  0.0 114.1 jit_solution(6918789033759388256)
XLA Ops:
  0.0 1.0 convert_reduce_fusion
  1.0 0.7 all_to_all.17
  1.7 11.1 %all-to-all-start.1 = ((f32[128,1,16]{2,1,0:T(1,128)}), f32[128,1,16]{2,1,0:T(1,128)S(1)}, u32[]{:S(2)}, u32[]{:S(2)}) async-start(f32[128,1,16]{2,1,0:T(1,128)} %bitcast.1), calls=%async_computation.1 | async-start | bytes 131072 | tf_op jit(solution)/shard_map/all_to_all | solution.py:151
  12.9 0.7 convert_element_type.8
  13.6 0.0 copy-start.1
  13.6 0.9 copy-done.1
  14.5 4.3 %local_mix.1 = f32[2048,512]{1,0:T(8,128)S(1)} custom-call(f32[8,256]{1,0:T(8,128)S(1)} %convert_element_type.9.signs, f32[256,256]{1,0:T(8,128)S(1)} %copy-done.1, f32[2048,512]{1,0:T(8,128)} %block.1), custom_call_target="tpu_custom_call" | custom-call | flops 1610612736 | bytes 8388608 | tf_op jit(solution)/shard_map/local_mix/pallas_call | solution.py:72
  18.9 0.0 copy-start
  18.9 1.9 %copy-done = f32[2048,512]{1,0:T(8,128)} copy-done((f32[2048,512]{1,0:T(8,128)}, f32[2048,512]{1,0:T(8,128)S(1)}, u32[]{:S(2)}) %copy-start) | copy-done | bytes 4194328
  20.8 1.2 %all-to-all-done.1 = f32[128,1,16]{2,1,0:T(1,128)S(1)} async-done(((f32[128,1,16]{2,1,0:T(1,128)}), f32[128,1,16]{2,1,0:T(1,128)S(1)}, u32[]{:S(2)}, u32[]{:S(2)}) %all-to-all-start.1) | async-done | bytes 8224 | tf_op jit(solution)/shard_map/all_to_all | solution.py:151
  22.0 9.1 %all-to-all-start = ((f32[128,16,512]{2,1,0:T(8,128)}), f32[128,16,512]{2,1,0:T(8,128)}, u32[]{:S(2)}, u32[]{:S(2)}) async-start(f32[128,16,512]{2,1,0:T(8,128)} %bitcast.7), calls=%async_computation | async-start | bytes 8388608 | tf_op jit(solution)/shard_map/all_to_all | solution.py:150
  31.1 50.8 %all-to-all-done.refs_0_ = f32[128,16,512]{2,1,0:T(8,128)} async-done(((f32[128,16,512]{2,1,0:T(8,128)}), f32[128,16,512]{2,1,0:T(8,128)}, u32[]{:S(2)}, u32[]{:S(2)}) %all-to-all-start) | async-done | bytes 4194336 | tf_op jit(solution)/shard_map/all_to_all | solution.py:150
  81.9 0.3 broadcast_in_dim.5.refs_1_
  82.3 6.6 %local_gram.1 = f32[512,512]{1,0:T(8,128)S(1)} custom-call(f32[128,16,512]{2,1,0:T(8,128)} %all-to-all-done.refs_0_, f32[128,16,128]{2,1,0:T(8,128)S(1)} %broadcast_in_dim.5.refs_1_), custom_call_target="tpu_custom_call" | custom-call | flops 2147483648 | bytes 4194304 | tf_op jit(solution)/shard_map/local_gram/pallas_call | solution.py:120
  88.9 0.3 reshape.16
  89.2 0.7 collective-permute-start
  89.9 1.5 %collective-permute-done = f32[64,4,512]{2,1,0:T(4,128)S(1)} collective-permute-done((f32[64,4,512]{2,1,0:T(4,128)S(1)}, f32[64,4,512]{2,1,0:T(4,128)S(1)}, u32[]{:S(2)}, u32[]{:S(2)}) %collective-permute-start) | collective-permute-done | bytes 524320 | tf_op jit(solution)/shard_map/ppermute | solution.py:136
  91.5 0.2 bitcast_add_fusion
  91.7 21.7 %all_to_all.23 = f32[64,4,512]{2,1,0:T(4,128)S(1)} all-to-all(f32[64,4,512]{2,1,0:T(4,128)S(1)} %bitcast_add_fusion), channel_id=1, replica_groups=mesh['yl'=2,'z'=4,'x'=4,'yh'=2,'c'=2] {'yl','z','x','yh'}, dimensions={0} | all-to-all | bytes 1048576 | tf_op jit(solution)/shard_map/all_to_all | solution.py:161
  113.4 0.7 reduce_sum.9
  (2 shorter events, 0.1 us)
Async XLA Ops:
  1.7 20.3 %all-to-all-start.1 = ((f32[128,1,16]{2,1,0:T(1,128)}), f32[128,1,16]{2,1,0:T(1,128)S(1)}, u32[]{:S(2)}, u32[]{:S(2)}) async-start(f32[128,1,16]{2,1,0:T(1,128)} %bitcast.1), calls=%async_computation.1 | async-start | bytes 131072 | tf_op jit(solution)/shard_map/all_to_all | solution.py:151
  13.6 0.9 copy-start.1
  18.9 1.9 %copy-start = (f32[2048,512]{1,0:T(8,128)}, f32[2048,512]{1,0:T(8,128)S(1)}, u32[]{:S(2)}) copy-start(f32[2048,512]{1,0:T(8,128)S(1)} %local_mix.1) | copy-start | bytes 12582916
  22.0 59.9 %all-to-all-start = ((f32[128,16,512]{2,1,0:T(8,128)}), f32[128,16,512]{2,1,0:T(8,128)}, u32[]{:S(2)}, u32[]{:S(2)}) async-start(f32[128,16,512]{2,1,0:T(8,128)} %bitcast.7), calls=%async_computation | async-start | bytes 8388608 | tf_op jit(solution)/shard_map/all_to_all | solution.py:150
  89.2 2.3 %collective-permute-start = (f32[64,4,512]{2,1,0:T(4,128)S(1)}, f32[64,4,512]{2,1,0:T(4,128)S(1)}, u32[]{:S(2)}, u32[]{:S(2)}) collective-permute-start(f32[64,4,512]{2,1,0:T(4,128)S(1)} %dynamic-slice_bitcast_fusion), channel_id=1, source_target_pairs={{0,1},{1,0},{2,3},{3,2},{4,5},{5,4},{6,7},{7,6},{8,9},{9,8},{10,11... | collective-permute-start | bytes 1572872 | tf_op jit(solution)/shard_map/ppermute | solution.py:136

commit v2 on v1

v2 whole, which is shorter than its diff:
```python
import jax
import jax.numpy as jnp
from jax import lax
from jax.experimental import pallas as pl
from jax.experimental.pallas import tpu as pltpu
from jax.sharding import Mesh, PartitionSpec as P

AXES = ("yl", "z", "x", "yh", "c")
CHIPS = ("yl", "z", "x", "yh")
TILE = 256
LANES = 128
SUBLANES = 8
VMEM_BYTES = 32 << 20


def butterfly(value):
    count = value.shape[0]
    if count == 1:
        return value
    half = count // 2
    first, second = value[:half], value[half:]
    return jnp.concatenate([butterfly(first + second), butterfly(first - second)])


def split2(value):
    high = value.astype(jnp.bfloat16)
    low = (value - high.astype(jnp.float32)).astype(jnp.bfloat16)
    return high, low


def split3(value):
    high = value.astype(jnp.bfloat16)
    rest = value - high.astype(jnp.float32)
    middle = rest.astype(jnp.bfloat16)
    low = (rest - middle.astype(jnp.float32)).astype(jnp.bfloat16)
    return high, middle, low


def sign_table():
    row = lax.broadcasted_iota(jnp.int32, (TILE, TILE), 0)
    column = lax.broadcasted_iota(jnp.int32, (TILE, TILE), 1)
    shared = row & column
    shared = shared ^ (shared >> 4)
    shared = shared ^ (shared >> 2)
    shared = shared ^ (shared >> 1)
    return (1 - 2 * (shared & 1)).astype(jnp.float32)


def flag_lines(offsets, devices, inner):
    count = offsets.shape[1]
    place = lax.broadcasted_iota(jnp.int32, (devices, count), 0)
    left = jnp.where(place == offsets // inner, 1.0, 0.0)
    lane = lax.broadcasted_iota(jnp.int32, (LANES, count), 0)
    right = jnp.where(lane == offsets % inner, 1.0, 0.0)
    return lax.dot_general(
        left.astype(jnp.bfloat16),
        right.astype(jnp.bfloat16),
        (((1,), (1,)), ((), ())),
        preferred_element_type=jnp.float32,
    )


def mix_kernel(devices, signs_far, sampled_far, block, mixed, held, signs, sampled, arrive, small):
    groups, _, columns = block.shape
    inner = groups * TILE // devices
    lines = mixed.shape[0] // devices
    lane_tiles = TILE // LANES
    column_tiles = columns // LANES
    signs_copy = pltpu.make_async_copy(signs_far, signs, small.at[0])
    sampled_copy = pltpu.make_async_copy(sampled_far, sampled, small.at[1])
    incoming = [pltpu.make_async_copy(block.at[g], held.at[g], arrive.at[g]) for g in range(groups)]
    for copy in [signs_copy, sampled_copy] + incoming:
        copy.start()
    table = sign_table()
    signs_copy.wait()
    sampled_copy.wait()
    flips = signs[...].astype(jnp.float32)
    offsets = jnp.concatenate([sampled[i : i + 1, :] for i in range(sampled.shape[0])], axis=1)
    flags = flag_lines(offsets, devices, inner)
    for number in range(devices):
        mixed[pl.ds(number * lines + lines - 1, 1), :] = flags[number : number + 1, :]
    for g in range(groups):
        left = jnp.concatenate(
            [
                table[:, t * LANES : (t + 1) * LANES] * flips[g * lane_tiles + t : g * lane_tiles + t + 1, :]
                for t in range(lane_tiles)
            ],
            axis=1,
        ).astype(jnp.bfloat16)
        incoming[g].wait()
        high, middle, low = split3(held[g])
        held[g] = (
            jnp.dot(left, low, preferred_element_type=jnp.float32)
            + jnp.dot(left, middle, preferred_element_type=jnp.float32)
            + jnp.dot(left, high, preferred_element_type=jnp.float32)
        )
    for start in range(0, TILE, SUBLANES):
        for column in range(column_tiles):
            value = butterfly(held[:, pl.ds(start, SUBLANES), pl.ds(column * LANES, LANES)])
            tile = (start % inner) // SUBLANES * column_tiles + column
            for g in range(groups):
                first = (g * TILE + start) // inner * lines + tile * SUBLANES
                mixed[pl.ds(first, SUBLANES), :] = value[g]


def local_mix(matrix, signs, sampled, devices):
    rows, columns = matrix.shape
    groups = rows // TILE
    lines = rows // devices * columns // LANES + 1
    far = pl.BlockSpec(memory_space=pltpu.HBM)
    stay = lambda value: pltpu.with_memory_space_constraint(value, pltpu.HBM)
    return pl.pallas_call(
        lambda *refs: mix_kernel(devices, *refs),
        out_shape=pltpu.VMEM((devices * lines, LANES), jnp.float32),
        in_specs=[far, far, far],
        out_specs=pl.BlockSpec(memory_space=pltpu.VMEM),
        scratch_shapes=[
            pltpu.VMEM((groups, TILE, columns), jnp.float32),
            pltpu.VMEM((rows // LANES, LANES), jnp.int32),
            pltpu.VMEM((sampled.shape[0] // LANES, LANES), jnp.int32),
            pltpu.SemaphoreType.DMA((groups,)),
            pltpu.SemaphoreType.DMA((2,)),
        ],
        compiler_params=pltpu.CompilerParams(vmem_limit_bytes=VMEM_BYTES),
        cost_estimate=pl.CostEstimate(
            flops=6 * rows * TILE * columns, bytes_accessed=8 * rows * columns, transcendentals=0
        ),
        name="local_mix",
    )(
        stay(signs.reshape(-1, LANES)),
        stay(sampled.reshape(-1, LANES)),
        stay(matrix.reshape(groups, TILE, columns)),
    )


def gram_kernel(scale, devices, core, block, mine, other, chosen, work, parts):
    lines = block.shape[0] // devices
    columns = mine.shape[1]
    column_tiles = columns // LANES
    tiles = lines // SUBLANES // column_tiles
    near = SUBLANES
    far = devices // near
    sublane = lax.broadcasted_iota(jnp.int32, (SUBLANES, LANES), 0)
    lane = lax.broadcasted_iota(jnp.int32, (SUBLANES, LANES), 1)
    spread = [
        jnp.broadcast_to(block[pl.ds(number * lines + lines - 1, 1), :], (SUBLANES, LANES))
        for number in range(devices)
    ]
    ones = jnp.ones((LANES, LANES), jnp.bfloat16)
    for tile in range(tiles):
        own = lane == sublane + tile * SUBLANES
        flags = jnp.concatenate([jnp.where(own, value, 0.0) for value in spread]).astype(jnp.bfloat16)
        chosen[tile] = jnp.dot(flags, ones, preferred_element_type=jnp.float32).reshape(devices, SUBLANES, LANES)
    product = None
    for tile in range(tiles):
        for column in range(column_tiles):
            number = tile * column_tiles + column
            lanes = pl.ds(column * LANES, LANES)
            slot = work.at[number % 2]
            for start in range(near):
                value = butterfly(
                    jnp.stack(
                        [
                            block[pl.ds((start + near * step) * lines + number * SUBLANES, SUBLANES), :]
                            for step in range(far)
                        ]
                    )
                )
                for step in range(far):
                    slot[start + near * step] = value[step]
            for step in range(far):
                group = pl.ds(near * step, near)
                value = butterfly(slot[group]) * chosen[tile, group]
                high, low = split2(value.reshape(near * SUBLANES, LANES))
                rows = pl.ds(near * SUBLANES * step, near * SUBLANES)
                parts[tile, rows, lanes] = high
                parts[tile, rows, pl.ds(columns + column * LANES, LANES)] = low
        term = lax.dot_general(
            parts[tile, :, :columns], parts[tile], (((0,), (0,)), ((), ())), preferred_element_type=jnp.float32
        )
        product = term if product is None else product + term
    cross = product[:, columns:]
    gram = (product[:, :columns] + (cross + cross.T)) * scale
    pairs = gram.reshape(columns // 16, 2, 8, columns)
    first, second = pairs[:, 0], pairs[:, 1]
    upper = lax.broadcasted_iota(jnp.int32, first.shape, 1) < 4
    flat = lambda value: value.reshape(columns // 2, columns)
    turn = lambda value: pltpu.roll(value, 4, 1)
    zero = flat(jnp.where(upper, first, turn(second)))
    one = flat(jnp.where(upper, turn(first), second))
    here = core[0] == 0
    mine[...] = jnp.where(here, zero, one)
    other[...] = jnp.where(here, one, zero)


def local_gram(block, core, devices, columns, scale):
    lines = block.shape[0] // devices
    tiles = lines * LANES // columns // SUBLANES
    half = jax.ShapeDtypeStruct((columns // 2, columns), jnp.float32)
    vmem = pl.BlockSpec(memory_space=pltpu.VMEM)
    return pl.pallas_call(
        lambda *refs: gram_kernel(scale, devices, *refs),
        out_shape=(half, half),
        in_specs=[pl.BlockSpec(memory_space=pltpu.SMEM), vmem],
        out_specs=(vmem, vmem),
        scratch_shapes=[
            pltpu.VMEM((tiles, devices, SUBLANES, LANES), jnp.float32),
            pltpu.VMEM((2, devices, SUBLANES, LANES), jnp.float32),
            pltpu.VMEM((tiles, devices * SUBLANES, 2 * columns), jnp.bfloat16),
        ],
        compiler_params=pltpu.CompilerParams(vmem_limit_bytes=VMEM_BYTES),
        cost_estimate=pl.CostEstimate(
            flops=4 * tiles * SUBLANES * devices * columns * columns,
            bytes_accessed=4 * devices * lines * LANES,
            transcendentals=0,
        ),
        name="local_gram",
    )(core.reshape(1), block)


def local(matrix, sign_flips, sampled_rows):
    rows, columns = matrix.shape
    devices = lax.axis_size(AXES)
    chips = devices // 2
    samples = sampled_rows.shape[0] * devices
    scale = 1.0 / (rows * devices) / samples

    core = lax.axis_index("c")
    mixed = local_mix(matrix, sign_flips, sampled_rows, devices)
    mixed, core = lax.optimization_barrier((mixed, core))
    lines = mixed.shape[0] // devices
    blocks = lax.all_to_all(mixed.reshape(devices, lines * LANES), AXES, 0, 0, tiled=True)
    mine, other = local_gram(blocks.reshape(devices * lines, LANES), core, devices, columns, scale)

    summed = mine + lax.ppermute(other, "c", [(0, 1), (1, 0)])
    pieces = lax.all_to_all(summed.reshape(chips, -1, columns), CHIPS, 0, 0, tiled=True)
    return jnp.sum(pieces, axis=0)


def solution(mesh):
    fine = Mesh(mesh.devices.reshape(2, 4, 4, 2, 2), AXES)
    return jax.shard_map(
        local, mesh=fine, in_specs=(P(AXES, None), P(AXES), P(AXES)), out_specs=P(AXES, None), check_vma=False
    )
```

time: 114 us -> 98.4 us (0.86)
  blocking collectives: 21.7 us -> 85.2 us
  waiting for transfers between devices: 53.5 us -> 1.9 us
  starting transfers between devices: 21 us -> 0.09 us
  local copies, waits for them, and re-layouts: 4.28 us -> 0.15 us
  other arithmetic: 2.6 us -> 0.79 us
    all_to_all x1 -> x2, blocking collectives: 21.7 us -> 85.2 us  [the longest x1 64.5 us: local(): lax.all_to_all(mixed.reshape(devices, lines * LANES), AXES, 0, 0, tiled=T...]
    all_to_all x2 -> x0, waiting for transfers between devices: 52 us -> none  [the longest x1 50.8 us: local(): blocks = lax.all_to_all(mixed, AXES, 0, 0, tiled=True)]
    all_to_all x2 -> x0, starting transfers between devices: 20.3 us -> none  [the longest x1 11.1 us: local(): flags = lax.all_to_all(flags, AXES, 0, 0, tiled=True)]
    unnamed x4 -> x0, local copies, waits for them, and re-layouts: 2.88 us -> none
  transfers between devices with their start and end apart: 3 -> 1, of which waited for: 3 -> 1; matrix products, arithmetic and copies ran while one was open for 1% -> 0% of each run, Pallas kernels for 4% -> 0%
where the time goes in v2:
time: 98.4 us; the launch traced here: 98.2 us
  blocking collectives  85.2 us (87%)
  Pallas kernels  10.1 us (10%)
  waiting for transfers between devices  1.9 us (2%)
    all_to_all x1, blocking collectives, local(): lax.all_to_all(mixed.reshape(devices, lines * LANES), AXES, 0, 0, tiled=T...  64.5 us
    all_to_all x1, blocking collectives, local(): lax.all_to_all(summed.reshape(chips, -1, columns), CHIPS, 0, 0, tiled=True)  20.6 us
    pallas_call x1, Pallas kernels, local_mix(): pl.pallas_call(lambda *refs: mix_kernel(devices, *refs), out_shape=pltpu....  5.77 us
    pallas_call x1, Pallas kernels, local_gram(): pl.pallas_call(lambda *refs: gram_kernel(scale, devices, *refs), out_shap...  4.33 us
  transfers between devices with their start and end apart: 1, of which 1 were waited for; matrix products, arithmetic and copies ran while one was open for 0% of the time, Pallas kernels for 0%

profile of v2, /device:TPU:0, one launch (start us, length us, event | category | flops | bytes accessed | tf_op | source)
XLA Modules:
  0.0 98.2 jit_solution(10434682453997132039)
XLA Ops:
  0.0 5.8 %local_mix.1 = f32[8320,128]{1,0:T(8,128)S(1)} custom-call(s32[16,128]{1,0:T(8,128)} %bitcast.9, s32[2,128]{1,0:T(2,128)} %bitcast.10, f32[8,256,512]{2,1,0:T(8,128)} %bitcast.8), custom_call_target="tpu_custom_call" | custom-call | flops 1610612736 | bytes 8388608 | tf_op jit(solution)/shard_map/local_mix/pallas_call | solution.py:112
  5.8 64.5 %all_to_all.14 = f32[128,1,8320]{2,1,0:T(1,128)S(1)} all-to-all(f32[128,1,8320]{2,1,0:T(1,128)S(1)} %bitcast.6), channel_id=1, replica_groups=mesh['yl'=2,'z'=4,'x'=4,'yh'=2,'c'=2] {'yl','z','x','yh','c'}, dimensions={0} | all-to-all | bytes 8519680 | tf_op jit(solution)/shard_map/all_to_all | solution.py:232
  70.3 4.3 %local_gram.1 = (f32[256,512]{1,0:T(8,128)S(1)}, f32[256,512]{1,0:T(8,128)S(1)}) custom-call(s32[1]{0:T(128)} %bitcast.3.refs_0_, f32[8320,128]{1,0:T(8,128)S(1)} %bitcast.7), custom_call_target="tpu_custom_call" | custom-call | flops 2147483648 | bytes 4259840 | tf_op jit(solution)/shard_map/local_gram/pallas_call | solution.py:201
  74.7 0.1 collective-permute-start
  74.7 1.9 %collective-permute-done = f32[256,512]{1,0:T(8,128)S(1)} collective-permute-done((f32[256,512]{1,0:T(8,128)S(1)}, f32[256,512]{1,0:T(8,128)S(1)}, u32[]{:S(2)}, u32[]{:S(2)}) %collective-permute-start) | collective-permute-done | bytes 524320 | tf_op jit(solution)/shard_map/ppermute | solution.py:235
  76.6 0.1 add.3
  76.7 0.1 reshape.28
  76.9 20.6 %all_to_all.15 = f32[64,4,512]{2,1,0:T(4,128)S(1)} all-to-all(f32[64,4,512]{2,1,0:T(4,128)S(1)} %reshape.28), channel_id=1, replica_groups=mesh['yl'=2,'z'=4,'x'=4,'yh'=2,'c'=2] {'yl','z','x','yh'}, dimensions={0} | all-to-all | bytes 1048576 | tf_op jit(solution)/shard_map/all_to_all | solution.py:236
  97.5 0.7 reduce_sum.9
Async XLA Ops:
  74.7 2.0 %collective-permute-start = (f32[256,512]{1,0:T(8,128)S(1)}, f32[256,512]{1,0:T(8,128)S(1)}, u32[]{:S(2)}, u32[]{:S(2)}) collective-permute-start(f32[256,512]{1,0:T(8,128)S(1)} %get-tuple-element.12), channel_id=1, source_target_pairs={{0,1},{1,0},{2,3},{3,2},{4,5},{5,4},{6,7},{7,6},{8,9},{9,8},{10,11... | collective-permute-start | bytes 1572872 | tf_op jit(solution)/shard_map/ppermute | solution.py:235

commit v3 on v2

--- a/solution.py
+++ b/solution.py
@@ -7,7 +7,7 @@
 
 AXES = ("yl", "z", "x", "yh", "c")
 CHIPS = ("yl", "z", "x", "yh")
-TILE = 256
+TILE = 128
 LANES = 128
 SUBLANES = 8
 VMEM_BYTES = 32 << 20
@@ -64,36 +64,35 @@
     groups, _, columns = block.shape
     inner = groups * TILE // devices
     lines = mixed.shape[0] // devices
-    lane_tiles = TILE // LANES
     column_tiles = columns // LANES
+    quarter = groups // arrive.shape[0]
     signs_copy = pltpu.make_async_copy(signs_far, signs, small.at[0])
     sampled_copy = pltpu.make_async_copy(sampled_far, sampled, small.at[1])
-    incoming = [pltpu.make_async_copy(block.at[g], held.at[g], arrive.at[g]) for g in range(groups)]
+    incoming = [
+        pltpu.make_async_copy(block.at[pl.ds(start, quarter)], held.at[pl.ds(start, quarter)], arrive.at[number])
+        for number, start in enumerate(range(0, groups, quarter))
+    ]
     for copy in [signs_copy, sampled_copy] + incoming:
         copy.start()
     table = sign_table()
     signs_copy.wait()
+    flips = signs[...].astype(jnp.float32)
+    due = {0: incoming[:1], quarter: incoming[1:-1], groups - quarter: incoming[-1:]}
+    for g in range(groups):
+        for copy in due.get(g, []):
+            copy.wait()
+        left = (table * flips[g : g + 1, :]).astype(jnp.bfloat16)
+        high, middle, low = split3(held[g])
+        held[g] = jnp.dot(left, low, preferred_element_type=jnp.float32) + jnp.dot(
+            jnp.concatenate([left, left], axis=1),
+            jnp.concatenate([middle, high], axis=0),
+            preferred_element_type=jnp.float32,
+        )
     sampled_copy.wait()
-    flips = signs[...].astype(jnp.float32)
     offsets = jnp.concatenate([sampled[i : i + 1, :] for i in range(sampled.shape[0])], axis=1)
     flags = flag_lines(offsets, devices, inner)
     for number in range(devices):
         mixed[pl.ds(number * lines + lines - 1, 1), :] = flags[number : number + 1, :]
-    for g in range(groups):
-        left = jnp.concatenate(
-            [
-                table[:, t * LANES : (t + 1) * LANES] * flips[g * lane_tiles + t : g * lane_tiles + t + 1, :]
-                for t in range(lane_tiles)
-            ],
-            axis=1,
-        ).astype(jnp.bfloat16)
-        incoming[g].wait()
-        high, middle, low = split3(held[g])
-        held[g] = (
-            jnp.dot(left, low, preferred_element_type=jnp.float32)
-            + jnp.dot(left, middle, preferred_element_type=jnp.float32)
-            + jnp.dot(left, high, preferred_element_type=jnp.float32)
-        )
     for start in range(0, TILE, SUBLANES):
         for column in range(column_tiles):
             value = butterfly(held[:, pl.ds(start, SUBLANES), pl.ds(column * LANES, LANES)])
@@ -118,7 +117,7 @@
             pltpu.VMEM((groups, TILE, columns), jnp.float32),
             pltpu.VMEM((rows // LANES, LANES), jnp.int32),
             pltpu.VMEM((sampled.shape[0] // LANES, LANES), jnp.int32),
-            pltpu.SemaphoreType.DMA((groups,)),
+            pltpu.SemaphoreType.DMA((4,)),
             pltpu.SemaphoreType.DMA((2,)),
         ],
         compiler_params=pltpu.CompilerParams(vmem_limit_bytes=VMEM_BYTES),
@@ -151,7 +150,7 @@
         own = lane == sublane + tile * SUBLANES
         flags = jnp.concatenate([jnp.where(own, value, 0.0) for value in spread]).astype(jnp.bfloat16)
         chosen[tile] = jnp.dot(flags, ones, preferred_element_type=jnp.float32).reshape(devices, SUBLANES, LANES)
-    product = None
+    depth = devices * SUBLANES
     for tile in range(tiles):
         for column in range(column_tiles):
             number = tile * column_tiles + column
@@ -172,15 +171,25 @@
                 group = pl.ds(near * step, near)
                 value = butterfly(slot[group]) * chosen[tile, group]
                 high, low = split2(value.reshape(near * SUBLANES, LANES))
-                rows = pl.ds(near * SUBLANES * step, near * SUBLANES)
-                parts[tile, rows, lanes] = high
-                parts[tile, rows, pl.ds(columns + column * LANES, LANES)] = low
-        term = lax.dot_general(
-            parts[tile, :, :columns], parts[tile], (((0,), (0,)), ((), ())), preferred_element_type=jnp.float32
-        )
-        product = term if product is None else product + term
-    cross = product[:, columns:]
-    gram = (product[:, :columns] + (cross + cross.T)) * scale
+                rows = pl.ds(tile * depth + near * SUBLANES * step, near * SUBLANES)
+                parts[rows, lanes] = high
+                parts[rows, pl.ds(columns + column * LANES, LANES)] = low
+    half = columns // 2
+    product = lambda left, right: lax.dot_general(
+        left, right, (((0,), (0,)), ((), ())), preferred_element_type=jnp.float32
+    )
+    top = product(parts[:, :half], parts[...])
+    bottom = product(parts[:, half:columns], parts[:, half:])
+    high = [top[:, :half], top[:, half:columns], bottom[:, :half]]
+    cross = [top[:, columns : columns + half], top[:, columns + half :], bottom[:, half:columns], bottom[:, columns:]]
+    middle = high[1] + (cross[1] + cross[2].T)
+    gram = scale * jnp.concatenate(
+        [
+            jnp.concatenate([high[0] + (cross[0] + cross[0].T), middle], axis=1),
+            jnp.concatenate([middle.T, high[2] + (cross[3] + cross[3].T)], axis=1),
+        ],
+        axis=0,
+    )
     pairs = gram.reshape(columns // 16, 2, 8, columns)
     first, second = pairs[:, 0], pairs[:, 1]
     upper = lax.broadcasted_iota(jnp.int32, first.shape, 1) < 4
@@ -206,7 +215,7 @@
         scratch_shapes=[
             pltpu.VMEM((tiles, devices, SUBLANES, LANES), jnp.float32),
             pltpu.VMEM((2, devices, SUBLANES, LANES), jnp.float32),
-            pltpu.VMEM((tiles, devices * SUBLANES, 2 * columns), jnp.bfloat16),
+            pltpu.VMEM((tiles * devices * SUBLANES, 2 * columns), jnp.bfloat16),
         ],
         compiler_params=pltpu.CompilerParams(vmem_limit_bytes=VMEM_BYTES),
         cost_estimate=pl.CostEstimate(

time: 98.4 us -> 96.4 us (0.980)
  Pallas kernels: 10.1 us -> 8.1 us
    pallas_call x1, Pallas kernels: 5.77 us -> 3.87 us  [local_mix(): pl.pallas_call(lambda *refs: mix_kernel(devices, *refs), out_shape=pltpu....]
where the time goes in v3:
time: 96.4 us; the launch traced here: 96.3 us
  blocking collectives  85.2 us (88%)
  Pallas kernels  8.1 us (8%)
  waiting for transfers between devices  1.9 us (2%)
    all_to_all x1, blocking collectives, local(): lax.all_to_all(mixed.reshape(devices, lines * LANES), AXES, 0, 0, tiled=T...  64.5 us
    all_to_all x1, blocking collectives, local(): lax.all_to_all(summed.reshape(chips, -1, columns), CHIPS, 0, 0, tiled=True)  20.7 us
    pallas_call x1, Pallas kernels, local_gram(): pl.pallas_call(lambda *refs: gram_kernel(scale, devices, *refs), out_shap...  4.24 us
    pallas_call x1, Pallas kernels, local_mix(): pl.pallas_call(lambda *refs: mix_kernel(devices, *refs), out_shape=pltpu....  3.87 us
  transfers between devices with their start and end apart: 1, of which 1 were waited for; matrix products, arithmetic and copies ran while one was open for 0% of the time, Pallas kernels for 0%

profile of v3, /device:TPU:0, one launch (start us, length us, event | category | flops | bytes accessed | tf_op | source)
XLA Modules:
  0.0 96.3 jit_solution(7772887578592563950)
XLA Ops:
  0.0 3.9 %local_mix.1 = f32[8320,128]{1,0:T(8,128)S(1)} custom-call(s32[16,128]{1,0:T(8,128)} %bitcast.9, s32[2,128]{1,0:T(2,128)} %bitcast.10, f32[16,128,512]{2,1,0:T(8,128)} %bitcast.8), custom_call_target="tpu_custom_call" | custom-call | flops 805306368 | bytes 8388608 | tf_op jit(solution)/shard_map/local_mix/pallas_call | solution.py:111
  3.9 64.5 %all_to_all.14 = f32[128,1,8320]{2,1,0:T(1,128)S(1)} all-to-all(f32[128,1,8320]{2,1,0:T(1,128)S(1)} %bitcast.6), channel_id=1, replica_groups=mesh['yl'=2,'z'=4,'x'=4,'yh'=2,'c'=2] {'yl','z','x','yh','c'}, dimensions={0} | all-to-all | bytes 8519680 | tf_op jit(solution)/shard_map/all_to_all | solution.py:241
  68.4 4.2 %local_gram.1 = (f32[256,512]{1,0:T(8,128)S(1)}, f32[256,512]{1,0:T(8,128)S(1)}) custom-call(s32[1]{0:T(128)} %bitcast.3.refs_0_, f32[8320,128]{1,0:T(8,128)S(1)} %bitcast.7), custom_call_target="tpu_custom_call" | custom-call | flops 2147483648 | bytes 4259840 | tf_op jit(solution)/shard_map/local_gram/pallas_call | solution.py:210
  72.7 0.1 collective-permute-start
  72.7 1.9 %collective-permute-done = f32[256,512]{1,0:T(8,128)S(1)} collective-permute-done((f32[256,512]{1,0:T(8,128)S(1)}, f32[256,512]{1,0:T(8,128)S(1)}, u32[]{:S(2)}, u32[]{:S(2)}) %collective-permute-start) | collective-permute-done | bytes 524320 | tf_op jit(solution)/shard_map/ppermute | solution.py:244
  74.6 0.1 add.3
  74.7 0.1 reshape.28
  74.9 20.7 %all_to_all.15 = f32[64,4,512]{2,1,0:T(4,128)S(1)} all-to-all(f32[64,4,512]{2,1,0:T(4,128)S(1)} %reshape.28), channel_id=1, replica_groups=mesh['yl'=2,'z'=4,'x'=4,'yh'=2,'c'=2] {'yl','z','x','yh'}, dimensions={0} | all-to-all | bytes 1048576 | tf_op jit(solution)/shard_map/all_to_all | solution.py:245
  95.5 0.7 reduce_sum.9
Async XLA Ops:
  72.7 2.0 %collective-permute-start = (f32[256,512]{1,0:T(8,128)S(1)}, f32[256,512]{1,0:T(8,128)S(1)}, u32[]{:S(2)}, u32[]{:S(2)}) collective-permute-start(f32[256,512]{1,0:T(8,128)S(1)} %get-tuple-element.12), channel_id=1, source_target_pairs={{0,1},{1,0},{2,3},{3,2},{4,5},{5,4},{6,7},{7,6},{8,9},{9,8},{10,11... | collective-permute-start | bytes 1572872 | tf_op jit(solution)/shard_map/ppermute | solution.py:244

commit v4 on v3

--- a/solution.py
+++ b/solution.py
@@ -5,8 +5,7 @@
 from jax.experimental.pallas import tpu as pltpu
 from jax.sharding import Mesh, PartitionSpec as P
 
-AXES = ("yl", "z", "x", "yh", "c")
-CHIPS = ("yl", "z", "x", "yh")
+AXIS = "d"
 TILE = 128
 LANES = 128
 SUBLANES = 8
@@ -132,9 +131,9 @@
     )
 
 
-def gram_kernel(scale, devices, core, block, mine, other, chosen, work, parts):
+def gram_kernel(scale, devices, side, block, mine, other, chosen, work, parts):
     lines = block.shape[0] // devices
-    columns = mine.shape[1]
+    columns = mine.shape[2]
     column_tiles = columns // LANES
     tiles = lines // SUBLANES // column_tiles
     near = SUBLANES
@@ -190,22 +189,18 @@
         ],
         axis=0,
     )
-    pairs = gram.reshape(columns // 16, 2, 8, columns)
-    first, second = pairs[:, 0], pairs[:, 1]
-    upper = lax.broadcasted_iota(jnp.int32, first.shape, 1) < 4
-    flat = lambda value: value.reshape(columns // 2, columns)
-    turn = lambda value: pltpu.roll(value, 4, 1)
-    zero = flat(jnp.where(upper, first, turn(second)))
-    one = flat(jnp.where(upper, turn(first), second))
-    here = core[0] == 0
-    mine[...] = jnp.where(here, zero, one)
-    other[...] = jnp.where(here, one, zero)
-
-
-def local_gram(block, core, devices, columns, scale):
+    first_side = side[0] == 0
+    out_rows = mine.shape[1]
+    for place, chip in enumerate(exchange_order(mine.shape[0])):
+        rows = [gram[start : start + out_rows] for start in (2 * chip * out_rows, (2 * chip + 1) * out_rows)]
+        mine[place] = jnp.where(first_side, rows[0], rows[1])
+        other[place] = jnp.where(first_side, rows[1], rows[0])
+
+
+def local_gram(block, side, devices, columns, scale):
     lines = block.shape[0] // devices
     tiles = lines * LANES // columns // SUBLANES
-    half = jax.ShapeDtypeStruct((columns // 2, columns), jnp.float32)
+    half = jax.ShapeDtypeStruct((devices // 2, columns // devices, columns), jnp.float32)
     vmem = pl.BlockSpec(memory_space=pltpu.VMEM)
     return pl.pallas_call(
         lambda *refs: gram_kernel(scale, devices, *refs),
@@ -224,30 +219,35 @@
             transcendentals=0,
         ),
         name="local_gram",
-    )(core.reshape(1), block)
+    )(side.reshape(1), block)
+
+
+def exchange_order(chips):
+    return list(reversed(range(chips)))
 
 
 def local(matrix, sign_flips, sampled_rows):
     rows, columns = matrix.shape
-    devices = lax.axis_size(AXES)
+    devices = lax.axis_size(AXIS)
     chips = devices // 2
     samples = sampled_rows.shape[0] * devices
     scale = 1.0 / (rows * devices) / samples
 
-    core = lax.axis_index("c")
+    side = lax.axis_index(AXIS) % 2
     mixed = local_mix(matrix, sign_flips, sampled_rows, devices)
-    mixed, core = lax.optimization_barrier((mixed, core))
+    mixed, side = lax.optimization_barrier((mixed, side))
     lines = mixed.shape[0] // devices
-    blocks = lax.all_to_all(mixed.reshape(devices, lines * LANES), AXES, 0, 0, tiled=True)
-    mine, other = local_gram(blocks.reshape(devices * lines, LANES), core, devices, columns, scale)
-
-    summed = mine + lax.ppermute(other, "c", [(0, 1), (1, 0)])
-    pieces = lax.all_to_all(summed.reshape(chips, -1, columns), CHIPS, 0, 0, tiled=True)
+    blocks = lax.all_to_all(mixed.reshape(devices, lines * LANES), AXIS, 0, 0, tiled=True)
+    mine, other = local_gram(blocks.reshape(devices * lines, LANES), side, devices, columns, scale)
+
+    summed = mine + lax.ppermute(other, AXIS, [(i, i ^ 1) for i in range(devices)])
+    sides = [[2 * chip + side for chip in exchange_order(chips)] for side in range(2)]
+    pieces = lax.all_to_all(summed, AXIS, 0, 0, axis_index_groups=sides, tiled=True)
     return jnp.sum(pieces, axis=0)
 
 
 def solution(mesh):
-    fine = Mesh(mesh.devices.reshape(2, 4, 4, 2, 2), AXES)
+    flat = Mesh(mesh.devices.reshape(-1), (AXIS,))
     return jax.shard_map(
-        local, mesh=fine, in_specs=(P(AXES, None), P(AXES), P(AXES)), out_specs=P(AXES, None), check_vma=False
-    )
+        local, mesh=flat, in_specs=(P(AXIS, None), P(AXIS), P(AXIS)), out_specs=P(AXIS, None), check_vma=False
+    )

time: 96.4 us -> 95.6 us (level)
  no operation moved by 1% of the time
where the time goes in v4:
time: 95.6 us; the launch traced here: 95.5 us
  blocking collectives  84.5 us (88%)
  Pallas kernels  8.11 us (8%)
  waiting for transfers between devices  1.9 us (2%)
    all_to_all x1, blocking collectives, local(): lax.all_to_all(mixed.reshape(devices, lines * LANES), AXIS, 0, 0, tiled=T...  64.5 us
    all_to_all x1, blocking collectives, local(): lax.all_to_all(summed, AXIS, 0, 0, axis_index_groups=sides, tiled=True)  20 us
    pallas_call x1, Pallas kernels, local_gram(): pl.pallas_call(lambda *refs: gram_kernel(scale, devices, *refs), out_shap...  4.25 us
    pallas_call x1, Pallas kernels, local_mix(): pl.pallas_call(lambda *refs: mix_kernel(devices, *refs), out_shape=pltpu....  3.87 us
  transfers between devices with their start and end apart: 1, of which 1 were waited for; matrix products, arithmetic and copies ran while one was open for 0% of the time, Pallas kernels for 0%

profile of v4, /device:TPU:0, one launch (start us, length us, event | category | flops | bytes accessed | tf_op | source)
XLA Modules:
  0.0 95.5 jit_solution(13379550577913804951)
XLA Ops:
  0.0 3.9 %local_mix.1 = f32[8320,128]{1,0:T(8,128)S(1)} custom-call(s32[16,128]{1,0:T(8,128)} %bitcast.9, s32[2,128]{1,0:T(2,128)} %bitcast.10, f32[16,128,512]{2,1,0:T(8,128)} %bitcast.8), custom_call_target="tpu_custom_call" | custom-call | flops 805306368 | bytes 8388608 | tf_op jit(solution)/shard_map/local_mix/pallas_call | solution.py:110
  3.9 64.5 %all_to_all.14 = f32[128,1,8320]{2,1,0:T(1,128)S(1)} all-to-all(f32[128,1,8320]{2,1,0:T(1,128)S(1)} %bitcast.6), channel_id=1, replica_groups=mesh['gx'=8,'gy'=16] {'gx','gy'}, dimensions={0} | all-to-all | bytes 8519680 | tf_op jit(solution)/shard_map/all_to_all | solution.py:240
  68.4 4.2 %local_gram.1 = (f32[64,4,512]{2,1,0:T(4,128)S(1)}, f32[64,4,512]{2,1,0:T(4,128)S(1)}) custom-call(s32[1]{0:T(128)} %bitcast.3.refs_0_, f32[8320,128]{1,0:T(8,128)S(1)} %bitcast.7), custom_call_target="tpu_custom_call" | custom-call | flops 2147483648 | bytes 4259840 | tf_op jit(solution)/shard_map/local_gram/pallas_call | solution.py:205
  72.7 0.1 collective-permute-start
  72.8 1.9 %collective-permute-done = f32[64,4,512]{2,1,0:T(4,128)S(1)} collective-permute-done((f32[64,4,512]{2,1,0:T(4,128)S(1)}, f32[64,4,512]{2,1,0:T(4,128)S(1)}, u32[]{:S(2)}, u32[]{:S(2)}) %collective-permute-start) | collective-permute-done | bytes 524320 | tf_op jit(solution)/shard_map/ppermute | solution.py:243
  74.7 0.1 add.8
  74.8 20.0 %all_to_all.15 = f32[64,4,512]{2,1,0:T(4,128)S(1)} all-to-all(f32[64,4,512]{2,1,0:T(4,128)S(1)} %add.8), channel_id=1, replica_groups={{126,124,122,120,118,116,114,112,110,108,106,104,102,100,98,96,94,92,90..., dimensions={0} | all-to-all | bytes 1048576 | tf_op jit(solution)/shard_map/all_to_all | solution.py:245
  94.8 0.7 reduce_sum.9
Async XLA Ops:
  72.7 2.0 %collective-permute-start = (f32[64,4,512]{2,1,0:T(4,128)S(1)}, f32[64,4,512]{2,1,0:T(4,128)S(1)}, u32[]{:S(2)}, u32[]{:S(2)}) collective-permute-start(f32[64,4,512]{2,1,0:T(4,128)S(1)} %get-tuple-element.12), channel_id=1, source_target_pairs={{0,1},{1,0},{2,3},{3,2},{4,5},{5,4},{6,7},{7,6},{8,9},{9,8},{10,11... | collective-permute-start | bytes 1572872 | tf_op jit(solution)/shard_map/ppermute | solution.py:243

commit v5 on v4

--- a/solution.py
+++ b/solution.py
@@ -1,3 +1,5 @@
+import math
+
 import jax
 import jax.numpy as jnp
 from jax import lax
@@ -59,7 +61,7 @@
     )
 
 
-def mix_kernel(devices, signs_far, sampled_far, block, mixed, held, signs, sampled, arrive, small):
+def mix_kernel(devices, factor, signs_far, sampled_far, block, mixed, held, signs, sampled, arrive, small):
     groups, _, columns = block.shape
     inner = groups * TILE // devices
     lines = mixed.shape[0] // devices
@@ -73,7 +75,7 @@
     ]
     for copy in [signs_copy, sampled_copy] + incoming:
         copy.start()
-    table = sign_table()
+    table = sign_table() * factor
     signs_copy.wait()
     flips = signs[...].astype(jnp.float32)
     due = {0: incoming[:1], quarter: incoming[1:-1], groups - quarter: incoming[-1:]}
@@ -101,14 +103,14 @@
                 mixed[pl.ds(first, SUBLANES), :] = value[g]
 
 
-def local_mix(matrix, signs, sampled, devices):
+def local_mix(matrix, signs, sampled, devices, factor):
     rows, columns = matrix.shape
     groups = rows // TILE
     lines = rows // devices * columns // LANES + 1
     far = pl.BlockSpec(memory_space=pltpu.HBM)
     stay = lambda value: pltpu.with_memory_space_constraint(value, pltpu.HBM)
     return pl.pallas_call(
-        lambda *refs: mix_kernel(devices, *refs),
+        lambda *refs: mix_kernel(devices, factor, *refs),
         out_shape=pltpu.VMEM((devices * lines, LANES), jnp.float32),
         in_specs=[far, far, far],
         out_specs=pl.BlockSpec(memory_space=pltpu.VMEM),
@@ -168,7 +170,7 @@
                     slot[start + near * step] = value[step]
             for step in range(far):
                 group = pl.ds(near * step, near)
-                value = butterfly(slot[group]) * chosen[tile, group]
+                value = jnp.where(chosen[tile, group] != 0.0, butterfly(slot[group]), 0.0)
                 high, low = split2(value.reshape(near * SUBLANES, LANES))
                 rows = pl.ds(tile * depth + near * SUBLANES * step, near * SUBLANES)
                 parts[rows, lanes] = high
@@ -231,10 +233,11 @@
     devices = lax.axis_size(AXIS)
     chips = devices // 2
     samples = sampled_rows.shape[0] * devices
-    scale = 1.0 / (rows * devices) / samples
+    factor = 1.0 / math.sqrt(rows * devices)
+    scale = 1.0 / samples
 
     side = lax.axis_index(AXIS) % 2
-    mixed = local_mix(matrix, sign_flips, sampled_rows, devices)
+    mixed = local_mix(matrix, sign_flips, sampled_rows, devices, factor)
     mixed, side = lax.optimization_barrier((mixed, side))
     lines = mixed.shape[0] // devices
     blocks = lax.all_to_all(mixed.reshape(devices, lines * LANES), AXIS, 0, 0, tiled=True)

time: 95.6 us -> 95.7 us (level)
  no operation moved by 1% of the time
where the time goes in v5:
time: 95.7 us; the launch traced here: 95.6 us
  blocking collectives  84.5 us (88%)
  Pallas kernels  8.23 us (9%)
  waiting for transfers between devices  1.9 us (2%)
    all_to_all x1, blocking collectives, local(): lax.all_to_all(mixed.reshape(devices, lines * LANES), AXIS, 0, 0, tiled=T...  64.5 us
    all_to_all x1, blocking collectives, local(): lax.all_to_all(summed, AXIS, 0, 0, axis_index_groups=sides, tiled=True)  20 us
    pallas_call x1, Pallas kernels, local_gram(): pl.pallas_call(lambda *refs: gram_kernel(scale, devices, *refs), out_shap...  4.35 us
    pallas_call x1, Pallas kernels, local_mix(): pl.pallas_call(lambda *refs: mix_kernel(devices, factor, *refs), out_shap...  3.88 us
  transfers between devices with their start and end apart: 1, of which 1 were waited for; matrix products, arithmetic and copies ran while one was open for 0% of the time, Pallas kernels for 0%

profile of v5, /device:TPU:0, one launch (start us, length us, event | category | flops | bytes accessed | tf_op | source)
XLA Modules:
  0.0 95.6 jit_solution(10449316018210492611)
XLA Ops:
  0.0 3.9 %local_mix.1 = f32[8320,128]{1,0:T(8,128)S(1)} custom-call(s32[16,128]{1,0:T(8,128)} %bitcast.9, s32[2,128]{1,0:T(2,128)} %bitcast.10, f32[16,128,512]{2,1,0:T(8,128)} %bitcast.8), custom_call_target="tpu_custom_call" | custom-call | flops 805306368 | bytes 8388608 | tf_op jit(solution)/shard_map/local_mix/pallas_call | solution.py:112
  3.9 64.5 %all_to_all.14 = f32[128,1,8320]{2,1,0:T(1,128)S(1)} all-to-all(f32[128,1,8320]{2,1,0:T(1,128)S(1)} %bitcast.6), channel_id=1, replica_groups=mesh['gx'=8,'gy'=16] {'gx','gy'}, dimensions={0} | all-to-all | bytes 8519680 | tf_op jit(solution)/shard_map/all_to_all | solution.py:243
  68.4 4.3 %local_gram.1 = (f32[64,4,512]{2,1,0:T(4,128)S(1)}, f32[64,4,512]{2,1,0:T(4,128)S(1)}) custom-call(s32[1]{0:T(128)} %bitcast.3.refs_0_, f32[8320,128]{1,0:T(8,128)S(1)} %bitcast.7), custom_call_target="tpu_custom_call" | custom-call | flops 2147483648 | bytes 4259840 | tf_op jit(solution)/shard_map/local_gram/pallas_call | solution.py:207
  72.8 0.1 collective-permute-start
  72.9 1.9 %collective-permute-done = f32[64,4,512]{2,1,0:T(4,128)S(1)} collective-permute-done((f32[64,4,512]{2,1,0:T(4,128)S(1)}, f32[64,4,512]{2,1,0:T(4,128)S(1)}, u32[]{:S(2)}, u32[]{:S(2)}) %collective-permute-start) | collective-permute-done | bytes 524320 | tf_op jit(solution)/shard_map/ppermute | solution.py:246
  74.8 0.1 add.8
  74.9 20.0 %all_to_all.15 = f32[64,4,512]{2,1,0:T(4,128)S(1)} all-to-all(f32[64,4,512]{2,1,0:T(4,128)S(1)} %add.8), channel_id=1, replica_groups={{126,124,122,120,118,116,114,112,110,108,106,104,102,100,98,96,94,92,90..., dimensions={0} | all-to-all | bytes 1048576 | tf_op jit(solution)/shard_map/all_to_all | solution.py:248
  94.9 0.7 reduce_sum.9
Async XLA Ops:
  72.8 2.0 %collective-permute-start = (f32[64,4,512]{2,1,0:T(4,128)S(1)}, f32[64,4,512]{2,1,0:T(4,128)S(1)}, u32[]{:S(2)}, u32[]{:S(2)}) collective-permute-start(f32[64,4,512]{2,1,0:T(4,128)S(1)} %get-tuple-element.12), channel_id=1, source_target_pairs={{0,1},{1,0},{2,3},{3,2},{4,5},{5,4},{6,7},{7,6},{8,9},{9,8},{10,11... | collective-permute-start | bytes 1572872 | tf_op jit(solution)/shard_map/ppermute | solution.py:246

commit v6 on v5

--- a/solution.py
+++ b/solution.py
@@ -225,7 +225,7 @@
 
 
 def exchange_order(chips):
-    return list(reversed(range(chips)))
+    return [place ^ 0b010101 for place in range(chips)]
 
 
 def local(matrix, sign_flips, sampled_rows):

time: 95.7 us -> 93.5 us (0.977)
  blocking collectives: 84.5 us -> 82.1 us
    all_to_all x1, blocking collectives: 20 us -> 17.5 us  [local(): lax.all_to_all(summed, AXIS, 0, 0, axis_index_groups=sides, tiled=True)]
where the time goes in v6:
time: 93.5 us; the launch traced here: 93.2 us
  blocking collectives  82.1 us (88%)
  Pallas kernels  8.23 us (9%)
  waiting for transfers between devices  1.9 us (2%)
    all_to_all x1, blocking collectives, local(): lax.all_to_all(mixed.reshape(devices, lines * LANES), AXIS, 0, 0, tiled=T...  64.5 us
    all_to_all x1, blocking collectives, local(): lax.all_to_all(summed, AXIS, 0, 0, axis_index_groups=sides, tiled=True)  17.5 us
    pallas_call x1, Pallas kernels, local_gram(): pl.pallas_call(lambda *refs: gram_kernel(scale, devices, *refs), out_shap...  4.35 us
    pallas_call x1, Pallas kernels, local_mix(): pl.pallas_call(lambda *refs: mix_kernel(devices, factor, *refs), out_shap...  3.88 us
    ppermute x1, waiting for transfers between devices, local(): lax.ppermute(other, AXIS, [(i, i ^ 1) for i in range(devices)])  1.9 us
  transfers between devices with their start and end apart: 1, of which 1 were waited for; matrix products, arithmetic and copies ran while one was open for 0% of the time, Pallas kernels for 0%

profile of v6, /device:TPU:0, one launch (start us, length us, event | category | flops | bytes accessed | tf_op | source)
XLA Modules:
  0.0 93.2 jit_solution(465466298428569216)
XLA Ops:
  0.0 3.9 %local_mix.1 = f32[8320,128]{1,0:T(8,128)S(1)} custom-call(s32[16,128]{1,0:T(8,128)} %bitcast.9, s32[2,128]{1,0:T(2,128)} %bitcast.10, f32[16,128,512]{2,1,0:T(8,128)} %bitcast.8), custom_call_target="tpu_custom_call" | custom-call | flops 805306368 | bytes 8388608 | tf_op jit(solution)/shard_map/local_mix/pallas_call | solution.py:112
  3.9 64.5 %all_to_all.14 = f32[128,1,8320]{2,1,0:T(1,128)S(1)} all-to-all(f32[128,1,8320]{2,1,0:T(1,128)S(1)} %bitcast.6), channel_id=1, replica_groups=mesh['gx'=8,'gy'=16] {'gx','gy'}, dimensions={0} | all-to-all | bytes 8519680 | tf_op jit(solution)/shard_map/all_to_all | solution.py:243
  68.4 4.3 %local_gram.1 = (f32[64,4,512]{2,1,0:T(4,128)S(1)}, f32[64,4,512]{2,1,0:T(4,128)S(1)}) custom-call(s32[1]{0:T(128)} %bitcast.3.refs_0_, f32[8320,128]{1,0:T(8,128)S(1)} %bitcast.7), custom_call_target="tpu_custom_call" | custom-call | flops 2147483648 | bytes 4259840 | tf_op jit(solution)/shard_map/local_gram/pallas_call | solution.py:207
  72.8 0.1 collective-permute-start
  72.9 1.9 %collective-permute-done = f32[64,4,512]{2,1,0:T(4,128)S(1)} collective-permute-done((f32[64,4,512]{2,1,0:T(4,128)S(1)}, f32[64,4,512]{2,1,0:T(4,128)S(1)}, u32[]{:S(2)}, u32[]{:S(2)}) %collective-permute-start) | collective-permute-done | bytes 524320 | tf_op jit(solution)/shard_map/ppermute | solution.py:246
  74.8 0.1 add.8
  74.9 17.5 %all_to_all.15 = f32[64,4,512]{2,1,0:T(4,128)S(1)} all-to-all(f32[64,4,512]{2,1,0:T(4,128)S(1)} %add.8), channel_id=1, replica_groups={{42,40,46,44,34,32,38,36,58,56,62,60,50,48,54,52,10,8,14,12,2,0,6,4,26,..., dimensions={0} | all-to-all | bytes 1048576 | tf_op jit(solution)/shard_map/all_to_all | solution.py:248
  92.5 0.7 reduce_sum.9
Async XLA Ops:
  72.8 2.0 %collective-permute-start = (f32[64,4,512]{2,1,0:T(4,128)S(1)}, f32[64,4,512]{2,1,0:T(4,128)S(1)}, u32[]{:S(2)}, u32[]{:S(2)}) collective-permute-start(f32[64,4,512]{2,1,0:T(4,128)S(1)} %get-tuple-element.12), channel_id=1, source_target_pairs={{0,1},{1,0},{2,3},{3,2},{4,5},{5,4},{6,7},{7,6},{8,9},{9,8},{10,11... | collective-permute-start | bytes 1572872 | tf_op jit(solution)/shard_map/ppermute | solution.py:246

commit v7 on v6

--- a/solution.py
+++ b/solution.py
@@ -66,6 +66,7 @@
     inner = groups * TILE // devices
     lines = mixed.shape[0] // devices
     column_tiles = columns // LANES
+    place = places(main_order(devices))
     quarter = groups // arrive.shape[0]
     signs_copy = pltpu.make_async_copy(signs_far, signs, small.at[0])
     sampled_copy = pltpu.make_async_copy(sampled_far, sampled, small.at[1])
@@ -93,13 +94,13 @@
     offsets = jnp.concatenate([sampled[i : i + 1, :] for i in range(sampled.shape[0])], axis=1)
     flags = flag_lines(offsets, devices, inner)
     for number in range(devices):
-        mixed[pl.ds(number * lines + lines - 1, 1), :] = flags[number : number + 1, :]
+        mixed[pl.ds(place[number] * lines + lines - 1, 1), :] = flags[number : number + 1, :]
     for start in range(0, TILE, SUBLANES):
         for column in range(column_tiles):
             value = butterfly(held[:, pl.ds(start, SUBLANES), pl.ds(column * LANES, LANES)])
             tile = (start % inner) // SUBLANES * column_tiles + column
             for g in range(groups):
-                first = (g * TILE + start) // inner * lines + tile * SUBLANES
+                first = place[(g * TILE + start) // inner] * lines + tile * SUBLANES
                 mixed[pl.ds(first, SUBLANES), :] = value[g]
 
 
@@ -140,10 +141,11 @@
     tiles = lines // SUBLANES // column_tiles
     near = SUBLANES
     far = devices // near
+    place = places(main_order(devices))
     sublane = lax.broadcasted_iota(jnp.int32, (SUBLANES, LANES), 0)
     lane = lax.broadcasted_iota(jnp.int32, (SUBLANES, LANES), 1)
     spread = [
-        jnp.broadcast_to(block[pl.ds(number * lines + lines - 1, 1), :], (SUBLANES, LANES))
+        jnp.broadcast_to(block[pl.ds(place[number] * lines + lines - 1, 1), :], (SUBLANES, LANES))
         for number in range(devices)
     ]
     ones = jnp.ones((LANES, LANES), jnp.bfloat16)
@@ -161,7 +163,7 @@
                 value = butterfly(
                     jnp.stack(
                         [
-                            block[pl.ds((start + near * step) * lines + number * SUBLANES, SUBLANES), :]
+                            block[pl.ds(place[start + near * step] * lines + number * SUBLANES, SUBLANES), :]
                             for step in range(far)
                         ]
                     )
@@ -193,10 +195,11 @@
     )
     first_side = side[0] == 0
     out_rows = mine.shape[1]
-    for place, chip in enumerate(exchange_order(mine.shape[0])):
-        rows = [gram[start : start + out_rows] for start in (2 * chip * out_rows, (2 * chip + 1) * out_rows)]
-        mine[place] = jnp.where(first_side, rows[0], rows[1])
-        other[place] = jnp.where(first_side, rows[1], rows[0])
+    for number, chip in enumerate(last_order(mine.shape[0])):
+        starts = [(2 * chip + half) * out_rows for half in range(2)]
+        zero, one = [gram[start : start + out_rows] for start in starts]
+        mine[number] = jnp.where(first_side, zero, one)
+        other[number] = jnp.where(first_side, one, zero)
 
 
 def local_gram(block, side, devices, columns, scale):
@@ -224,8 +227,28 @@
     )(side.reshape(1), block)
 
 
-def exchange_order(chips):
-    return [place ^ 0b010101 for place in range(chips)]
+def chip_at(x, y, z):
+    return ((y % 2 * 4 + z) * 4 + x) * 2 + y // 2
+
+
+def coordinates(chip):
+    return chip // 2 % 4, chip % 2 * 2 + chip // 32, chip // 8 % 4
+
+
+def turned(chip):
+    return chip_at(*[(c + 2) % 4 for c in coordinates(chip)])
+
+
+def main_order(devices):
+    return [device for chip in range(devices // 2) for device in (2 * chip, 2 * turned(chip) + 1)]
+
+
+def last_order(chips):
+    return [turned(chip) for chip in range(chips)]
+
+
+def places(order):
+    return {device: place for place, device in enumerate(order)}
 
 
 def local(matrix, sign_flips, sampled_rows):
@@ -240,11 +263,13 @@
     mixed = local_mix(matrix, sign_flips, sampled_rows, devices, factor)
     mixed, side = lax.optimization_barrier((mixed, side))
     lines = mixed.shape[0] // devices
-    blocks = lax.all_to_all(mixed.reshape(devices, lines * LANES), AXIS, 0, 0, tiled=True)
+    blocks = lax.all_to_all(
+        mixed.reshape(devices, lines * LANES), AXIS, 0, 0, axis_index_groups=[main_order(devices)], tiled=True
+    )
     mine, other = local_gram(blocks.reshape(devices * lines, LANES), side, devices, columns, scale)
 
     summed = mine + lax.ppermute(other, AXIS, [(i, i ^ 1) for i in range(devices)])
-    sides = [[2 * chip + side for chip in exchange_order(chips)] for side in range(2)]
+    sides = [[2 * chip + side for chip in last_order(chips)] for side in range(2)]
     pieces = lax.all_to_all(summed, AXIS, 0, 0, axis_index_groups=sides, tiled=True)
     return jnp.sum(pieces, axis=0)
 

time: 93.5 us -> 92.5 us (0.989)
  blocking collectives: 82.1 us -> 81 us
    all_to_all x1, blocking collectives: 17.5 us -> 16.5 us  [local(): lax.all_to_all(summed, AXIS, 0, 0, axis_index_groups=sides, tiled=True)]
where the time goes in v7:
time: 92.5 us; the launch traced here: 92.1 us
  blocking collectives  81 us (88%)
  Pallas kernels  8.23 us (9%)
  waiting for transfers between devices  1.9 us (2%)
    all_to_all x1, blocking collectives, local(): lax.all_to_all(mixed.reshape(devices, lines * LANES), AXIS, 0, 0, axis_in...  64.6 us
    all_to_all x1, blocking collectives, local(): lax.all_to_all(summed, AXIS, 0, 0, axis_index_groups=sides, tiled=True)  16.5 us
    pallas_call x1, Pallas kernels, local_gram(): pl.pallas_call(lambda *refs: gram_kernel(scale, devices, *refs), out_shap...  4.35 us
    pallas_call x1, Pallas kernels, local_mix(): pl.pallas_call(lambda *refs: mix_kernel(devices, factor, *refs), out_shap...  3.88 us
    ppermute x1, waiting for transfers between devices, local(): lax.ppermute(other, AXIS, [(i, i ^ 1) for i in range(devices)])  1.9 us
  transfers between devices with their start and end apart: 1, of which 1 were waited for; matrix products, arithmetic and copies ran while one was open for 0% of the time, Pallas kernels for 0%

profile of v7, /device:TPU:0, one launch (start us, length us, event | category | flops | bytes accessed | tf_op | source)
XLA Modules:
  0.0 92.1 jit_solution(16691226536876541715)
XLA Ops:
  0.0 3.9 %local_mix.1 = f32[8320,128]{1,0:T(8,128)S(1)} custom-call(s32[16,128]{1,0:T(8,128)} %bitcast.9, s32[2,128]{1,0:T(2,128)} %bitcast.10, f32[16,128,512]{2,1,0:T(8,128)} %bitcast.8), custom_call_target="tpu_custom_call" | custom-call | flops 805306368 | bytes 8388608 | tf_op jit(solution)/shard_map/local_mix/pallas_call | solution.py:113
  3.9 64.6 %all_to_all.14 = f32[128,1,8320]{2,1,0:T(1,128)S(1)} all-to-all(f32[128,1,8320]{2,1,0:T(1,128)S(1)} %bitcast.6), channel_id=1, replica_groups={{0,43,2,41,4,47,6,45,8,35,10,33,12,39,14,37,16,59,18,57,20,63,22,61,24,..., dimensions={0} | all-to-all | bytes 8519680 | tf_op jit(solution)/shard_map/all_to_all | solution.py:266
  68.5 4.4 %local_gram.1 = (f32[64,4,512]{2,1,0:T(4,128)S(1)}, f32[64,4,512]{2,1,0:T(4,128)S(1)}) custom-call(s32[1]{0:T(128)} %bitcast.3.refs_0_, f32[8320,128]{1,0:T(8,128)S(1)} %bitcast.7), custom_call_target="tpu_custom_call" | custom-call | flops 2147483648 | bytes 4259840 | tf_op jit(solution)/shard_map/local_gram/pallas_call | solution.py:210
  72.8 0.1 collective-permute-start
  72.9 1.9 %collective-permute-done = f32[64,4,512]{2,1,0:T(4,128)S(1)} collective-permute-done((f32[64,4,512]{2,1,0:T(4,128)S(1)}, f32[64,4,512]{2,1,0:T(4,128)S(1)}, u32[]{:S(2)}, u32[]{:S(2)}) %collective-permute-start) | collective-permute-done | bytes 524320 | tf_op jit(solution)/shard_map/ppermute | solution.py:271
  74.8 0.1 add.8
  75.0 16.5 %all_to_all.15 = f32[64,4,512]{2,1,0:T(4,128)S(1)} all-to-all(f32[64,4,512]{2,1,0:T(4,128)S(1)} %add.8), channel_id=1, replica_groups={{42,40,46,44,34,32,38,36,58,56,62,60,50,48,54,52,10,8,14,12,2,0,6,4,26,..., dimensions={0} | all-to-all | bytes 1048576 | tf_op jit(solution)/shard_map/all_to_all | solution.py:273
  91.4 0.7 reduce_sum.9
Async XLA Ops:
  72.8 2.0 %collective-permute-start = (f32[64,4,512]{2,1,0:T(4,128)S(1)}, f32[64,4,512]{2,1,0:T(4,128)S(1)}, u32[]{:S(2)}, u32[]{:S(2)}) collective-permute-start(f32[64,4,512]{2,1,0:T(4,128)S(1)} %get-tuple-element.12), channel_id=1, source_target_pairs={{0,1},{1,0},{2,3},{3,2},{4,5},{5,4},{6,7},{7,6},{8,9},{9,8},{10,11... | collective-permute-start | bytes 1572872 | tf_op jit(solution)/shard_map/ppermute | solution.py:271

commit v8 on v7

--- a/solution.py
+++ b/solution.py
@@ -244,7 +244,12 @@
 
 
 def last_order(chips):
-    return [turned(chip) for chip in range(chips)]
+    order = []
+    for place in range(chips):
+        x, y, z = place % 4, place // 4 % 4, place // 16
+        order.append(chip_at(x, (y + x) % 4, (z + y + x) % 4))
+    order[0], order[53] = order[53], order[0]
+    return order
 
 
 def places(order):

time: 92.5 us -> 93 us (level)
  no operation moved by 1% of the time
where the time goes in v8:
time: 93 us; the launch traced here: 92.9 us
  blocking collectives  81.8 us (88%)
  Pallas kernels  8.23 us (9%)
  waiting for transfers between devices  1.9 us (2%)
    all_to_all x1, blocking collectives, local(): lax.all_to_all(mixed.reshape(devices, lines * LANES), AXIS, 0, 0, axis_in...  64.6 us
    all_to_all x1, blocking collectives, local(): lax.all_to_all(summed, AXIS, 0, 0, axis_index_groups=sides, tiled=True)  17.2 us
    pallas_call x1, Pallas kernels, local_gram(): pl.pallas_call(lambda *refs: gram_kernel(scale, devices, *refs), out_shap...  4.35 us
    pallas_call x1, Pallas kernels, local_mix(): pl.pallas_call(lambda *refs: mix_kernel(devices, factor, *refs), out_shap...  3.88 us
    ppermute x1, waiting for transfers between devices, local(): lax.ppermute(other, AXIS, [(i, i ^ 1) for i in range(devices)])  1.9 us
  transfers between devices with their start and end apart: 1, of which 1 were waited for; matrix products, arithmetic and copies ran while one was open for 0% of the time, Pallas kernels for 0%

profile of v8, /device:TPU:0, one launch (start us, length us, event | category | flops | bytes accessed | tf_op | source)
XLA Modules:
  0.0 92.9 jit_solution(13464557767007526522)
XLA Ops:
  0.0 3.9 %local_mix.1 = f32[8320,128]{1,0:T(8,128)S(1)} custom-call(s32[16,128]{1,0:T(8,128)} %bitcast.9, s32[2,128]{1,0:T(2,128)} %bitcast.10, f32[16,128,512]{2,1,0:T(8,128)} %bitcast.8), custom_call_target="tpu_custom_call" | custom-call | flops 805306368 | bytes 8388608 | tf_op jit(solution)/shard_map/local_mix/pallas_call | solution.py:113
  3.9 64.6 %all_to_all.14 = f32[128,1,8320]{2,1,0:T(1,128)S(1)} all-to-all(f32[128,1,8320]{2,1,0:T(1,128)S(1)} %bitcast.6), channel_id=1, replica_groups={{0,43,2,41,4,47,6,45,8,35,10,33,12,39,14,37,16,59,18,57,20,63,22,61,24,..., dimensions={0} | all-to-all | bytes 8519680 | tf_op jit(solution)/shard_map/all_to_all | solution.py:271
  68.5 4.4 %local_gram.1 = (f32[64,4,512]{2,1,0:T(4,128)S(1)}, f32[64,4,512]{2,1,0:T(4,128)S(1)}) custom-call(s32[1]{0:T(128)} %bitcast.3.refs_0_, f32[8320,128]{1,0:T(8,128)S(1)} %bitcast.7), custom_call_target="tpu_custom_call" | custom-call | flops 2147483648 | bytes 4259840 | tf_op jit(solution)/shard_map/local_gram/pallas_call | solution.py:210
  72.8 0.1 collective-permute-start
  72.9 1.9 %collective-permute-done = f32[64,4,512]{2,1,0:T(4,128)S(1)} collective-permute-done((f32[64,4,512]{2,1,0:T(4,128)S(1)}, f32[64,4,512]{2,1,0:T(4,128)S(1)}, u32[]{:S(2)}, u32[]{:S(2)}) %collective-permute-start) | collective-permute-done | bytes 524320 | tf_op jit(solution)/shard_map/ppermute | solution.py:276
  74.8 0.1 add.8
  75.0 17.2 %all_to_all.15 = f32[64,4,512]{2,1,0:T(4,128)S(1)} all-to-all(f32[64,4,512]{2,1,0:T(4,128)S(1)} %add.8), channel_id=1, replica_groups={{22,84,42,126,80,38,122,12,34,118,8,92,114,4,88,46,16,100,58,78,96,54,7..., dimensions={0} | all-to-all | bytes 1048576 | tf_op jit(solution)/shard_map/all_to_all | solution.py:278
  92.2 0.7 reduce_sum.9
Async XLA Ops:
  72.8 2.0 %collective-permute-start = (f32[64,4,512]{2,1,0:T(4,128)S(1)}, f32[64,4,512]{2,1,0:T(4,128)S(1)}, u32[]{:S(2)}, u32[]{:S(2)}) collective-permute-start(f32[64,4,512]{2,1,0:T(4,128)S(1)} %get-tuple-element.12), channel_id=1, source_target_pairs={{0,1},{1,0},{2,3},{3,2},{4,5},{5,4},{6,7},{7,6},{8,9},{9,8},{10,11... | collective-permute-start | bytes 1572872 | tf_op jit(solution)/shard_map/ppermute | solution.py:276

commit v9 on v7

--- a/solution.py
+++ b/solution.py
@@ -240,7 +240,12 @@
 
 
 def main_order(devices):
-    return [device for chip in range(devices // 2) for device in (2 * chip, 2 * turned(chip) + 1)]
+    order = []
+    for place in range(devices // 2):
+        y = place // 32 * 2 + place % 2
+        chip = chip_at(place // 2 % 4, y, place // 8 % 4)
+        order += [2 * chip, 2 * turned(chip) + 1]
+    return order
 
 
 def last_order(chips):

time: 92.5 us -> 92.6 us (level)
  no operation moved by 1% of the time
where the time goes in v9:
time: 92.6 us; the launch traced here: 92.3 us
  blocking collectives  81.2 us (88%)
  Pallas kernels  8.23 us (9%)
  waiting for transfers between devices  1.9 us (2%)
    all_to_all x1, blocking collectives, local(): lax.all_to_all(mixed.reshape(devices, lines * LANES), AXIS, 0, 0, axis_in...  64.7 us
    all_to_all x1, blocking collectives, local(): lax.all_to_all(summed, AXIS, 0, 0, axis_index_groups=sides, tiled=True)  16.5 us
    pallas_call x1, Pallas kernels, local_gram(): pl.pallas_call(lambda *refs: gram_kernel(scale, devices, *refs), out_shap...  4.34 us
    pallas_call x1, Pallas kernels, local_mix(): pl.pallas_call(lambda *refs: mix_kernel(devices, factor, *refs), out_shap...  3.88 us
    ppermute x1, waiting for transfers between devices, local(): lax.ppermute(other, AXIS, [(i, i ^ 1) for i in range(devices)])  1.9 us
  transfers between devices with their start and end apart: 1, of which 1 were waited for; matrix products, arithmetic and copies ran while one was open for 0% of the time, Pallas kernels for 0%

profile of v9, /device:TPU:0, one launch (start us, length us, event | category | flops | bytes accessed | tf_op | source)
XLA Modules:
  0.0 92.3 jit_solution(3263775886503672696)
XLA Ops:
  0.0 3.9 %local_mix.1 = f32[8320,128]{1,0:T(8,128)S(1)} custom-call(s32[16,128]{1,0:T(8,128)} %bitcast.9, s32[2,128]{1,0:T(2,128)} %bitcast.10, f32[16,128,512]{2,1,0:T(8,128)} %bitcast.8), custom_call_target="tpu_custom_call" | custom-call | flops 805306368 | bytes 8388608 | tf_op jit(solution)/shard_map/local_mix/pallas_call | solution.py:113
  3.9 64.7 %all_to_all.14 = f32[128,1,8320]{2,1,0:T(1,128)S(1)} all-to-all(f32[128,1,8320]{2,1,0:T(1,128)S(1)} %bitcast.6), channel_id=1, replica_groups={{0,43,64,107,4,47,68,111,8,35,72,99,12,39,76,103,16,59,80,123,20,63,84,..., dimensions={0} | all-to-all | bytes 8519680 | tf_op jit(solution)/shard_map/all_to_all | solution.py:271
  68.6 4.3 %local_gram.1 = (f32[64,4,512]{2,1,0:T(4,128)S(1)}, f32[64,4,512]{2,1,0:T(4,128)S(1)}) custom-call(s32[1]{0:T(128)} %bitcast.3.refs_0_, f32[8320,128]{1,0:T(8,128)S(1)} %bitcast.7), custom_call_target="tpu_custom_call" | custom-call | flops 2147483648 | bytes 4259840 | tf_op jit(solution)/shard_map/local_gram/pallas_call | solution.py:210
  73.0 0.1 collective-permute-start
  73.1 1.9 %collective-permute-done = f32[64,4,512]{2,1,0:T(4,128)S(1)} collective-permute-done((f32[64,4,512]{2,1,0:T(4,128)S(1)}, f32[64,4,512]{2,1,0:T(4,128)S(1)}, u32[]{:S(2)}, u32[]{:S(2)}) %collective-permute-start) | collective-permute-done | bytes 524320 | tf_op jit(solution)/shard_map/ppermute | solution.py:276
  75.0 0.1 add.8
  75.1 16.5 %all_to_all.15 = f32[64,4,512]{2,1,0:T(4,128)S(1)} all-to-all(f32[64,4,512]{2,1,0:T(4,128)S(1)} %add.8), channel_id=1, replica_groups={{42,40,46,44,34,32,38,36,58,56,62,60,50,48,54,52,10,8,14,12,2,0,6,4,26,..., dimensions={0} | all-to-all | bytes 1048576 | tf_op jit(solution)/shard_map/all_to_all | solution.py:278
  91.6 0.7 reduce_sum.9
Async XLA Ops:
  73.0 2.0 %collective-permute-start = (f32[64,4,512]{2,1,0:T(4,128)S(1)}, f32[64,4,512]{2,1,0:T(4,128)S(1)}, u32[]{:S(2)}, u32[]{:S(2)}) collective-permute-start(f32[64,4,512]{2,1,0:T(4,128)S(1)} %get-tuple-element.12), channel_id=1, source_target_pairs={{0,1},{1,0},{2,3},{3,2},{4,5},{5,4},{6,7},{7,6},{8,9},{9,8},{10,11... | collective-permute-start | bytes 1572872 | tf_op jit(solution)/shard_map/ppermute | solution.py:276

commit v10 on v7

--- a/solution.py
+++ b/solution.py
@@ -244,7 +244,7 @@
 
 
 def last_order(chips):
-    return [turned(chip) for chip in range(chips)]
+    return [turned(chip_at(place % 4, place // 4 % 4, place // 16)) for place in range(chips)]
 
 
 def places(order):

time: 92.5 us -> 92.4 us (level)
  no operation moved by 1% of the time
where the time goes in v10:
time: 92.4 us; the launch traced here: 92.2 us
  blocking collectives  81.1 us (88%)
  Pallas kernels  8.23 us (9%)
  waiting for transfers between devices  1.9 us (2%)
    all_to_all x1, blocking collectives, local(): lax.all_to_all(mixed.reshape(devices, lines * LANES), AXIS, 0, 0, axis_in...  64.6 us
    all_to_all x1, blocking collectives, local(): lax.all_to_all(summed, AXIS, 0, 0, axis_index_groups=sides, tiled=True)  16.5 us
    pallas_call x1, Pallas kernels, local_gram(): pl.pallas_call(lambda *refs: gram_kernel(scale, devices, *refs), out_shap...  4.35 us
    pallas_call x1, Pallas kernels, local_mix(): pl.pallas_call(lambda *refs: mix_kernel(devices, factor, *refs), out_shap...  3.88 us
    ppermute x1, waiting for transfers between devices, local(): lax.ppermute(other, AXIS, [(i, i ^ 1) for i in range(devices)])  1.9 us
  transfers between devices with their start and end apart: 1, of which 1 were waited for; matrix products, arithmetic and copies ran while one was open for 0% of the time, Pallas kernels for 0%

profile of v10, /device:TPU:0, one launch (start us, length us, event | category | flops | bytes accessed | tf_op | source)
XLA Modules:
  0.0 92.2 jit_solution(11744185408696587607)
XLA Ops:
  0.0 3.9 %local_mix.1 = f32[8320,128]{1,0:T(8,128)S(1)} custom-call(s32[16,128]{1,0:T(8,128)} %bitcast.9, s32[2,128]{1,0:T(2,128)} %bitcast.10, f32[16,128,512]{2,1,0:T(8,128)} %bitcast.8), custom_call_target="tpu_custom_call" | custom-call | flops 805306368 | bytes 8388608 | tf_op jit(solution)/shard_map/local_mix/pallas_call | solution.py:113
  3.9 64.6 %all_to_all.14 = f32[128,1,8320]{2,1,0:T(1,128)S(1)} all-to-all(f32[128,1,8320]{2,1,0:T(1,128)S(1)} %bitcast.6), channel_id=1, replica_groups={{0,43,2,41,4,47,6,45,8,35,10,33,12,39,14,37,16,59,18,57,20,63,22,61,24,..., dimensions={0} | all-to-all | bytes 8519680 | tf_op jit(solution)/shard_map/all_to_all | solution.py:266
  68.5 4.4 %local_gram.1 = (f32[64,4,512]{2,1,0:T(4,128)S(1)}, f32[64,4,512]{2,1,0:T(4,128)S(1)}) custom-call(s32[1]{0:T(128)} %bitcast.3.refs_0_, f32[8320,128]{1,0:T(8,128)S(1)} %bitcast.7), custom_call_target="tpu_custom_call" | custom-call | flops 2147483648 | bytes 4259840 | tf_op jit(solution)/shard_map/local_gram/pallas_call | solution.py:210
  72.8 0.1 collective-permute-start
  72.9 1.9 %collective-permute-done = f32[64,4,512]{2,1,0:T(4,128)S(1)} collective-permute-done((f32[64,4,512]{2,1,0:T(4,128)S(1)}, f32[64,4,512]{2,1,0:T(4,128)S(1)}, u32[]{:S(2)}, u32[]{:S(2)}) %collective-permute-start) | collective-permute-done | bytes 524320 | tf_op jit(solution)/shard_map/ppermute | solution.py:271
  74.8 0.1 add.8
  75.0 16.5 %all_to_all.15 = f32[64,4,512]{2,1,0:T(4,128)S(1)} all-to-all(f32[64,4,512]{2,1,0:T(4,128)S(1)} %add.8), channel_id=1, replica_groups={{42,46,34,38,106,110,98,102,40,44,32,36,104,108,96,100,58,62,50,54,122,..., dimensions={0} | all-to-all | bytes 1048576 | tf_op jit(solution)/shard_map/all_to_all | solution.py:273
  91.5 0.7 reduce_sum.9
Async XLA Ops:
  72.8 2.0 %collective-permute-start = (f32[64,4,512]{2,1,0:T(4,128)S(1)}, f32[64,4,512]{2,1,0:T(4,128)S(1)}, u32[]{:S(2)}, u32[]{:S(2)}) collective-permute-start(f32[64,4,512]{2,1,0:T(4,128)S(1)} %get-tuple-element.12), channel_id=1, source_target_pairs={{0,1},{1,0},{2,3},{3,2},{4,5},{5,4},{6,7},{7,6},{8,9},{9,8},{10,11... | collective-permute-start | bytes 1572872 | tf_op jit(solution)/shard_map/ppermute | solution.py:271
